TPU v7x, 32 devices: a whole 2x2x4 slice. The times are simulated.
32 devices in a mesh: gx: 8 (over y, x, core), gy: 4 (over z).
Axes of the slice: x: 2, y: 2, z: 4, core: 2. Of those that a mesh axis runs over, the one named last changes fastest.
Arguments:
- right_side: float32 [32, 32, 512], P('gx', 'gy'), may hold values from -18 to 18
- labels: int32 [32, 32, 512], P('gx', 'gy'), may hold values from 0 to 2
- conduct_table: float32 [3], replicated, may hold values from 0.2 to 5
Outputs:
- correction: float32 [32, 32, 512], P('gx', 'gy')
All inputs are finite; a program needn't handle non-finite values.
Results may differ from a plain program's by a relative error of at most 0.0003.
Values sent between devices are 32-bit elements; how exact they have to be, the bound alone decides.
A program may use at most 128 MiB of HBM per device.

v0:
```python
import jax
import jax.numpy as jnp
from jax import lax
from jax.sharding import PartitionSpec as P

SWEEPS = 8


OMEGA = 0.8


def extended(cells, sides, width):
    for axis, dim in sides:
        count = lax.axis_size(axis)
        ends = count - 1
        head = lax.slice_in_dim(cells, 0, width, axis=dim)
        tail = lax.slice_in_dim(cells, cells.shape[dim] - width, cells.shape[dim], axis=dim)
        cells = jnp.concatenate(
            [
                lax.ppermute(tail, axis, [(i, (i + 1) % count) for i in range(ends)]),
                cells,
                lax.ppermute(head, axis, [((i + 1) % count, i) for i in range(ends)]),
            ],
            axis=dim,
        )
    return cells


def lookup(labels, table):
    return jnp.where(labels == 0, table[0], jnp.where(labels == 1, table[1], table[2]))


def face_couplings(padded):
    own = padded[1:-1, 1:-1, 1:-1]
    own = jnp.where(own > 0.0, own, 1.0)

    def across(beside):
        beside = jnp.where(beside > 0.0, beside, own)
        return 2.0 * (own * beside) / (own + beside)

    return jnp.stack(
        [
            across(padded[:-2, 1:-1, 1:-1]),
            across(padded[2:, 1:-1, 1:-1]),
            across(padded[1:-1, :-2, 1:-1]),
            across(padded[1:-1, 2:, 1:-1]),
            across(padded[1:-1, 1:-1, :-2]),
            across(padded[1:-1, 1:-1, 2:]),
        ]
    )


def coupled(couplings, padded):
    total = couplings[0] * padded[:-2, 1:-1, 1:-1] + couplings[1] * padded[2:, 1:-1, 1:-1]
    total = total + couplings[2] * padded[1:-1, :-2, 1:-1] + couplings[3] * padded[1:-1, 2:, 1:-1]
    total = total + couplings[4] * padded[1:-1, 1:-1, :-2] + couplings[5] * padded[1:-1, 1:-1, 2:]
    return total


def relax(couplings, diagonal, source, field, padded):
    image = diagonal * field - coupled(couplings, padded)
    return field + OMEGA * (source - image) / diagonal


def residual_of(couplings, diagonal, source, field, padded):
    return source - (diagonal * field - coupled(couplings, padded))


def coarsen_couplings(couplings):
    extent = couplings.shape
    blocks = couplings.reshape(6, extent[1] // 2, 2, extent[2] // 2, 2, extent[3] // 2, 2)
    lower_one = jnp.sum(blocks[0][:, 0], axis=(2, 4))
    upper_one = jnp.sum(blocks[1][:, 1], axis=(2, 4))
    lower_two = jnp.sum(blocks[2][:, :, :, 0], axis=(1, 4))
    upper_two = jnp.sum(blocks[3][:, :, :, 1], axis=(1, 4))
    lower_three = jnp.sum(blocks[4][..., 0], axis=(1, 3))
    upper_three = jnp.sum(blocks[5][..., 1], axis=(1, 3))
    return jnp.stack([lower_one, upper_one, lower_two, upper_two, lower_three, upper_three])


def restrict(field):
    extent = field.shape
    return jnp.sum(
        field.reshape(extent[0] // 2, 2, extent[1] // 2, 2, extent[2] // 2, 2), axis=(1, 3, 5)
    )


def prolong(field):
    extent = field.shape
    spread = jnp.broadcast_to(
        field[:, None, :, None, :, None], (extent[0], 2, extent[1], 2, extent[2], 2)
    )
    return spread.reshape(2 * extent[0], 2 * extent[1], 2 * extent[2])


def pad_third(field):
    return jnp.pad(field, ((0, 0), (0, 0), (1, 1)))


def with_rim(field, level):
    if level == 0:
        padded = extended(field, (("gx", 0), ("gy", 1)), 1)
    elif level == 1:
        padded = extended(field, (("gx", 0), ("gy", 1)), 1)
    else:
        padded = extended(field, (("gx", 0), ("gy", 1)), 1)
    return pad_third(padded)


def from_zero(couplings, diagonal, source):
    empty = jnp.zeros_like(source)
    return relax(couplings, diagonal, source, empty, jnp.pad(empty, 1))


def shards(right_side, labels, conduct_table):
    conduct = lookup(labels, conduct_table)
    conduct_padded = extended(conduct, (("gx", 0), ("gy", 1)), 1)
    fine_couplings = face_couplings(pad_third(conduct_padded))
    fine_diagonal = jnp.sum(fine_couplings, axis=0)
    first_iterate = from_zero(fine_couplings, fine_diagonal, right_side)
    first_padded = pad_third(extended(first_iterate, (("gx", 0), ("gy", 1)), 1))
    fine_iterate = relax(fine_couplings, fine_diagonal, right_side, first_iterate, first_padded)
    fine_residual = residual_of(
        fine_couplings, fine_diagonal, right_side, fine_iterate, with_rim(fine_iterate, 0)
    )
    middle_source = restrict(fine_residual)
    middle_couplings = coarsen_couplings(fine_couplings)
    middle_diagonal = jnp.sum(middle_couplings, axis=0)
    middle_iterate = from_zero(middle_couplings, middle_diagonal, middle_source)
    middle_iterate = relax(
        middle_couplings,
        middle_diagonal,
        middle_source,
        middle_iterate,
        with_rim(middle_iterate, 1),
    )
    middle_residual = residual_of(
        middle_couplings,
        middle_diagonal,
        middle_source,
        middle_iterate,
        with_rim(middle_iterate, 1),
    )
    coarse_source = restrict(middle_residual)
    coarse_couplings = coarsen_couplings(middle_couplings)
    coarse_diagonal = jnp.sum(coarse_couplings, axis=0)
    coarse_iterate = from_zero(coarse_couplings, coarse_diagonal, coarse_source)
    for repeat in range(SWEEPS - 1):
        coarse_iterate = relax(
            coarse_couplings,
            coarse_diagonal,
            coarse_source,
            coarse_iterate,
            with_rim(coarse_iterate, 2),
        )
    middle_iterate = middle_iterate + prolong(coarse_iterate)
    middle_iterate = relax(
        middle_couplings,
        middle_diagonal,
        middle_source,
        middle_iterate,
        with_rim(middle_iterate, 1),
    )
    fine_iterate = fine_iterate + prolong(middle_iterate)
    return relax(fine_couplings, fine_diagonal, right_side, fine_iterate, with_rim(fine_iterate, 0))


def solution(mesh):
    in_specs = (P("gx", "gy", None), P("gx", "gy", None), P())
    out_specs = P("gx", "gy", None)
    return jax.shard_map(shards, mesh=mesh, in_specs=in_specs, out_specs=out_specs, check_vma=False)
```

profile of v0, /device:TPU:0, one launch (start us, length us, event | category | flops | bytes accessed | tf_op | source)
XLA Modules:
  0.0 280.2 jit_solution(10091483235407069994)
XLA Ops:
  1.4 2.8 select_select_fusion
  4.2 2.4 collective-permute-start
  7.8 3.9 %collective-permute-done.1 = f32[1,8,512]{2,1,0:T(8,128)S(1)} collective-permute-done((f32[1,8,512]{2,1,0:T(8,128)S(1)}, f32[1,8,512]{2,1,0:T(8,128)S(1)}, u32[]{:S(2)}, u32[]{:S(2)}) %collective-permute-start.1) | collective-permute-done | bytes 16416 | tf_op jit(solution)/shard_map/ppermute | solution.py:22
  11.7 3.5 %collective-permute-start.2 = (f32[6,1,512]{2,1,0:T(1,128)S(1)}, f32[6,1,512]{2,1,0:T(1,128)S(1)}, u32[]{:S(2)}, u32[]{:S(2)}) collective-permute-start(f32[6,1,512]{2,1,0:T(1,128)S(1)} %get-tuple-element.18), channel_id=1, source_target_pairs={{0,1},{1,2},{2,3},{4,5},{5,6},{6,7},{8,9},{9,10},{10,11},{12,13},{... | collective-permute-start | bytes 36872 | tf_op jit(solution)/shard_map/ppermute | solution.py:20
  16.6 4.2 %collective-permute-done.3 = f32[6,1,512]{2,1,0:T(1,128)S(1)} collective-permute-done((f32[6,1,512]{2,1,0:T(1,128)S(1)}, f32[6,1,512]{2,1,0:T(1,128)S(1)}, u32[]{:S(2)}, u32[]{:S(2)}) %collective-permute-start.3) | collective-permute-done | bytes 12320 | tf_op jit(solution)/shard_map/ppermute | solution.py:22
  22.1 5.6 %squeeze.64 = f32[2,2,4,2,256,2]{5,4,3,2,1,0:T(8,128)} reshape(f32[4,8,512]{2,1,0:T(8,128)S(1)} %get-tuple-element.7) | data formatting | bytes 131072 | tf_op jit(solution)/shard_map/squeeze | solution.py:76
  27.7 5.5 %squeeze.65 = f32[2,2,4,2,256,2]{5,4,3,2,1,0:T(8,128)} reshape(f32[4,8,512]{2,1,0:T(8,128)S(1)} %get-tuple-element.6) | data formatting | bytes 131072 | tf_op jit(solution)/shard_map/squeeze | solution.py:77
  33.2 5.5 %squeeze.62 = f32[2,2,4,2,256,2]{5,4,3,2,1,0:T(8,128)} reshape(f32[4,8,512]{2,1,0:T(8,128)S(1)} %get-tuple-element.9) | data formatting | bytes 131072 | tf_op jit(solution)/shard_map/squeeze | solution.py:74
  38.7 5.6 %squeeze.63 = f32[2,2,4,2,256,2]{5,4,3,2,1,0:T(8,128)} reshape(f32[4,8,512]{2,1,0:T(8,128)S(1)} %get-tuple-element.8) | data formatting | bytes 131072 | tf_op jit(solution)/shard_map/squeeze | solution.py:75
  44.3 2.9 %collective-permute-start.4 = (f32[1,8,512]{2,1,0:T(8,128)S(1)}, f32[1,8,512]{2,1,0:T(8,128)S(1)}, u32[]{:S(2)}, u32[]{:S(2)}) collective-permute-start(f32[1,8,512]{2,1,0:T(8,128)S(1)} %get-tuple-element.24), channel_id=1, source_target_pairs={{0,4},{4,8},{8,12},{12,16},{16,20},{20,24},{24,28},{1,5},{5,9},{9,... | collective-permute-start | bytes 49160 | tf_op jit(solution)/shard_map/ppermute | solution.py:20
  48.8 5.9 %slice_reduce_fusion = (f32[2,4,256]{2,1,0:T(4,128)S(1)}, f32[2,4,256]{2,1,0:T(4,128)S(1)}) fusion(f32[2,2,4,2,256,2]{5,4,3,2,1,0:T(8,128)} %squeeze.65, f32[2,2,4,2,256,2]{5,4,3,2,1,0:T(8,128)} %squeeze.64), kind=kLoop, calls=%fused_computation | loop fusion | flops 12288 | bytes 81920 | tf_op jit(solution)/shard_map/reduce_sum | solution.py:77
  55.3 5.6 %squeeze.60 = f32[2,2,4,2,256,2]{5,4,3,2,1,0:T(8,128)} reshape(f32[4,8,512]{2,1,0:T(8,128)S(1)} %get-tuple-element.11) | data formatting | bytes 131072 | tf_op jit(solution)/shard_map/squeeze | solution.py:72
  61.0 5.5 %squeeze.61 = f32[2,2,4,2,256,2]{5,4,3,2,1,0:T(8,128)} reshape(f32[4,8,512]{2,1,0:T(8,128)S(1)} %get-tuple-element.10) | data formatting | bytes 131072 | tf_op jit(solution)/shard_map/squeeze | solution.py:73
  66.5 3.5 %collective-permute-start.6 = (f32[6,1,512]{2,1,0:T(1,128)S(1)}, f32[6,1,512]{2,1,0:T(1,128)S(1)}, u32[]{:S(2)}, u32[]{:S(2)}) collective-permute-start(f32[6,1,512]{2,1,0:T(1,128)S(1)} %get-tuple-element.16), channel_id=1, source_target_pairs={{0,1},{1,2},{2,3},{4,5},{5,6},{6,7},{8,9},{9,10},{10,11},{12,13},{... | collective-permute-start | bytes 36872 | tf_op jit(solution)/shard_map/ppermute | solution.py:20
  71.3 2.8 %slice_reduce_fusion.4 = (f32[2,4,256]{2,1,0:T(4,128)S(1)}, f32[2,4,256]{2,1,0:T(4,128)S(1)}) fusion(f32[2,2,4,2,256,2]{5,4,3,2,1,0:T(8,128)} %squeeze.61, f32[2,2,4,2,256,2]{5,4,3,2,1,0:T(8,128)} %squeeze.60), kind=kLoop, calls=%fused_computation.4 | loop fusion | flops 12288 | bytes 81920 | tf_op jit(solution)/shard_map/reduce_sum | solution.py:73
  75.9 2.3 collective-permute-start.8
  80.5 3.2 %collective-permute-done.9 = f32[1,8,512]{2,1,0:T(8,128)S(1)} collective-permute-done((f32[1,8,512]{2,1,0:T(8,128)S(1)}, f32[1,8,512]{2,1,0:T(8,128)S(1)}, u32[]{:S(2)}, u32[]{:S(2)}) %collective-permute-start.9) | collective-permute-done | bytes 16416 | tf_op jit(solution)/shard_map/ppermute | solution.py:22
  83.7 3.6 %collective-permute-start.10 = (f32[6,1,512]{2,1,0:T(1,128)S(1)}, f32[6,1,512]{2,1,0:T(1,128)S(1)}, u32[]{:S(2)}, u32[]{:S(2)}) collective-permute-start(f32[6,1,512]{2,1,0:T(1,128)S(1)} %get-tuple-element.14), channel_id=1, source_target_pairs={{0,1},{1,2},{2,3},{4,5},{5,6},{6,7},{8,9},{9,10},{10,11},{12,13},{... | collective-permute-start | bytes 36872 | tf_op jit(solution)/shard_map/ppermute | solution.py:20
  89.2 3.7 %collective-permute-done.11 = f32[6,1,512]{2,1,0:T(1,128)S(1)} collective-permute-done((f32[6,1,512]{2,1,0:T(1,128)S(1)}, f32[6,1,512]{2,1,0:T(1,128)S(1)}, u32[]{:S(2)}, u32[]{:S(2)}) %collective-permute-start.11) | collective-permute-done | bytes 12320 | tf_op jit(solution)/shard_map/ppermute | solution.py:22
  93.2 5.5 %reshape.181 = f32[2,2,4,2,256,2]{5,4,3,2,1,0:T(8,128)} reshape(f32[4,8,512]{2,1,0:T(8,128)S(1)} %fusion.56) | data formatting | bytes 131072 | tf_op jit(solution)/shard_map/reshape | solution.py:84
  98.8 2.5 reduce_sum.269
  101.4 3.0 %collective-permute-start.12 = (f32[1,4,256]{2,1,0:T(4,128)S(1)}, f32[1,4,256]{2,1,0:T(4,128)S(1)}, u32[]{:S(2)}, u32[]{:S(2)}) collective-permute-start(f32[1,4,256]{2,1,0:T(4,128)S(1)} %get-tuple-element.38), channel_id=1, source_target_pairs={{0,4},{4,8},{8,12},{12,16},{16,20},{20,24},{24,28},{1,5},{5,9},{9,... | collective-permute-start | bytes 12296 | tf_op jit(solution)/shard_map/ppermute | solution.py:20
  106.3 2.9 %collective-permute-done.13 = f32[1,4,256]{2,1,0:T(4,128)S(1)} collective-permute-done((f32[1,4,256]{2,1,0:T(4,128)S(1)}, f32[1,4,256]{2,1,0:T(4,128)S(1)}, u32[]{:S(2)}, u32[]{:S(2)}) %collective-permute-start.13) | collective-permute-done | bytes 4128 | tf_op jit(solution)/shard_map/ppermute | solution.py:22
  109.2 3.5 %collective-permute-start.14 = (f32[4,1,256]{2,1,0:T(1,128)S(1)}, f32[4,1,256]{2,1,0:T(1,128)S(1)}, u32[]{:S(2)}, u32[]{:S(2)}) collective-permute-start(f32[4,1,256]{2,1,0:T(1,128)S(1)} %get-tuple-element.32), channel_id=1, source_target_pairs={{0,1},{1,2},{2,3},{4,5},{5,6},{6,7},{8,9},{9,10},{10,11},{12,13},{... | collective-permute-start | bytes 12296 | tf_op jit(solution)/shard_map/ppermute | solution.py:20
  114.6 3.6 %collective-permute-done.15 = f32[4,1,256]{2,1,0:T(1,128)S(1)} collective-permute-done((f32[4,1,256]{2,1,0:T(1,128)S(1)}, f32[4,1,256]{2,1,0:T(1,128)S(1)}, u32[]{:S(2)}, u32[]{:S(2)}) %collective-permute-start.15) | collective-permute-done | bytes 4128 | tf_op jit(solution)/shard_map/ppermute | solution.py:22
  118.4 3.0 %collective-permute-start.16 = (f32[1,4,256]{2,1,0:T(4,128)S(1)}, f32[1,4,256]{2,1,0:T(4,128)S(1)}, u32[]{:S(2)}, u32[]{:S(2)}) collective-permute-start(f32[1,4,256]{2,1,0:T(4,128)S(1)} %get-tuple-element.36), channel_id=1, source_target_pairs={{0,4},{4,8},{8,12},{12,16},{16,20},{20,24},{24,28},{1,5},{5,9},{9,... | collective-permute-start | bytes 12296 | tf_op jit(solution)/shard_map/ppermute | solution.py:20
  123.3 2.9 %collective-permute-done.17 = f32[1,4,256]{2,1,0:T(4,128)S(1)} collective-permute-done((f32[1,4,256]{2,1,0:T(4,128)S(1)}, f32[1,4,256]{2,1,0:T(4,128)S(1)}, u32[]{:S(2)}, u32[]{:S(2)}) %collective-permute-start.17) | collective-permute-done | bytes 4128 | tf_op jit(solution)/shard_map/ppermute | solution.py:22
  126.3 1.9 collective-permute-start.18
  129.6 4.1 %collective-permute-done.19 = f32[4,1,256]{2,1,0:T(1,128)S(1)} collective-permute-done((f32[4,1,256]{2,1,0:T(1,128)S(1)}, f32[4,1,256]{2,1,0:T(1,128)S(1)}, u32[]{:S(2)}, u32[]{:S(2)}) %collective-permute-start.19) | collective-permute-done | bytes 4128 | tf_op jit(solution)/shard_map/ppermute | solution.py:22
  134.3 3.2 %collective-permute-start.20 = (f32[1,2,128]{2,1,0:T(2,128)S(1)}, f32[1,2,128]{2,1,0:T(2,128)S(1)}, u32[]{:S(2)}, u32[]{:S(2)}) collective-permute-start(f32[1,2,128]{2,1,0:T(2,128)S(1)} %fusion.206), channel_id=1, source_target_pairs={{0,4},{4,8},{8,12},{12,16},{16,20},{20,24},{24,28},{1,5},{5,9},{9,... | collective-permute-start | bytes 3080 | tf_op jit(solution)/shard_map/ppermute | solution.py:20
  138.8 3.2 %collective-permute-done.21 = f32[1,2,128]{2,1,0:T(2,128)S(1)} collective-permute-done((f32[1,2,128]{2,1,0:T(2,128)S(1)}, f32[1,2,128]{2,1,0:T(2,128)S(1)}, u32[]{:S(2)}, u32[]{:S(2)}) %collective-permute-start.21) | collective-permute-done | bytes 1056 | tf_op jit(solution)/shard_map/ppermute | solution.py:22
  142.1 1.9 collective-permute-start.22
  145.3 4.2 %collective-permute-done.23 = f32[3,1,128]{2,1,0:T(1,128)S(1)} collective-permute-done((f32[3,1,128]{2,1,0:T(1,128)S(1)}, f32[3,1,128]{2,1,0:T(1,128)S(1)}, u32[]{:S(2)}, u32[]{:S(2)}) %collective-permute-start.23) | collective-permute-done | bytes 1568 | tf_op jit(solution)/shard_map/ppermute | solution.py:22
  149.7 3.2 %collective-permute-start.24 = (f32[1,2,128]{2,1,0:T(2,128)S(1)}, f32[1,2,128]{2,1,0:T(2,128)S(1)}, u32[]{:S(2)}, u32[]{:S(2)}) collective-permute-start(f32[1,2,128]{2,1,0:T(2,128)S(1)} %divide_add_fusion.5), channel_id=1, source_target_pairs={{0,4},{4,8},{8,12},{12,16},{16,20},{20,24},{24,28},{1,5},{5,9},{9,... | collective-permute-start | bytes 3080 | tf_op jit(solution)/shard_map/ppermute | solution.py:20
  154.2 3.2 %collective-permute-done.25 = f32[1,2,128]{2,1,0:T(2,128)S(1)} collective-permute-done((f32[1,2,128]{2,1,0:T(2,128)S(1)}, f32[1,2,128]{2,1,0:T(2,128)S(1)}, u32[]{:S(2)}, u32[]{:S(2)}) %collective-permute-start.25) | collective-permute-done | bytes 1056 | tf_op jit(solution)/shard_map/ppermute | solution.py:22
  157.4 1.9 collective-permute-start.26
  160.7 4.2 %collective-permute-done.27 = f32[3,1,128]{2,1,0:T(1,128)S(1)} collective-permute-done((f32[3,1,128]{2,1,0:T(1,128)S(1)}, f32[3,1,128]{2,1,0:T(1,128)S(1)}, u32[]{:S(2)}, u32[]{:S(2)}) %collective-permute-start.27) | collective-permute-done | bytes 1568 | tf_op jit(solution)/shard_map/ppermute | solution.py:22
  165.0 3.2 %collective-permute-start.28 = (f32[1,2,128]{2,1,0:T(2,128)S(1)}, f32[1,2,128]{2,1,0:T(2,128)S(1)}, u32[]{:S(2)}, u32[]{:S(2)}) collective-permute-start(f32[1,2,128]{2,1,0:T(2,128)S(1)} %divide_add_fusion.4), channel_id=1, source_target_pairs={{0,4},{4,8},{8,12},{12,16},{16,20},{20,24},{24,28},{1,5},{5,9},{9,... | collective-permute-start | bytes 3080 | tf_op jit(solution)/shard_map/ppermute | solution.py:20
  169.5 3.2 %collective-permute-done.29 = f32[1,2,128]{2,1,0:T(2,128)S(1)} collective-permute-done((f32[1,2,128]{2,1,0:T(2,128)S(1)}, f32[1,2,128]{2,1,0:T(2,128)S(1)}, u32[]{:S(2)}, u32[]{:S(2)}) %collective-permute-start.29) | collective-permute-done | bytes 1056 | tf_op jit(solution)/shard_map/ppermute | solution.py:22
  172.7 1.9 collective-permute-start.30
  176.0 4.2 %collective-permute-done.31 = f32[3,1,128]{2,1,0:T(1,128)S(1)} collective-permute-done((f32[3,1,128]{2,1,0:T(1,128)S(1)}, f32[3,1,128]{2,1,0:T(1,128)S(1)}, u32[]{:S(2)}, u32[]{:S(2)}) %collective-permute-start.31) | collective-permute-done | bytes 1568 | tf_op jit(solution)/shard_map/ppermute | solution.py:22
  180.3 3.2 %collective-permute-start.32 = (f32[1,2,128]{2,1,0:T(2,128)S(1)}, f32[1,2,128]{2,1,0:T(2,128)S(1)}, u32[]{:S(2)}, u32[]{:S(2)}) collective-permute-start(f32[1,2,128]{2,1,0:T(2,128)S(1)} %divide_add_fusion.3), channel_id=1, source_target_pairs={{0,4},{4,8},{8,12},{12,16},{16,20},{20,24},{24,28},{1,5},{5,9},{9,... | collective-permute-start | bytes 3080 | tf_op jit(solution)/shard_map/ppermute | solution.py:20
  184.8 3.2 %collective-permute-done.33 = f32[1,2,128]{2,1,0:T(2,128)S(1)} collective-permute-done((f32[1,2,128]{2,1,0:T(2,128)S(1)}, f32[1,2,128]{2,1,0:T(2,128)S(1)}, u32[]{:S(2)}, u32[]{:S(2)}) %collective-permute-start.33) | collective-permute-done | bytes 1056 | tf_op jit(solution)/shard_map/ppermute | solution.py:22
  188.1 1.9 collective-permute-start.34
  191.3 4.2 %collective-permute-done.35 = f32[3,1,128]{2,1,0:T(1,128)S(1)} collective-permute-done((f32[3,1,128]{2,1,0:T(1,128)S(1)}, f32[3,1,128]{2,1,0:T(1,128)S(1)}, u32[]{:S(2)}, u32[]{:S(2)}) %collective-permute-start.35) | collective-permute-done | bytes 1568 | tf_op jit(solution)/shard_map/ppermute | solution.py:22
  195.7 3.2 %collective-permute-start.36 = (f32[1,2,128]{2,1,0:T(2,128)S(1)}, f32[1,2,128]{2,1,0:T(2,128)S(1)}, u32[]{:S(2)}, u32[]{:S(2)}) collective-permute-start(f32[1,2,128]{2,1,0:T(2,128)S(1)} %divide_add_fusion.2), channel_id=1, source_target_pairs={{0,4},{4,8},{8,12},{12,16},{16,20},{20,24},{24,28},{1,5},{5,9},{9,... | collective-permute-start | bytes 3080 | tf_op jit(solution)/shard_map/ppermute | solution.py:20
  200.2 3.2 %collective-permute-done.37 = f32[1,2,128]{2,1,0:T(2,128)S(1)} collective-permute-done((f32[1,2,128]{2,1,0:T(2,128)S(1)}, f32[1,2,128]{2,1,0:T(2,128)S(1)}, u32[]{:S(2)}, u32[]{:S(2)}) %collective-permute-start.37) | collective-permute-done | bytes 1056 | tf_op jit(solution)/shard_map/ppermute | solution.py:22
  206.6 4.2 %collective-permute-done.39 = f32[3,1,128]{2,1,0:T(1,128)S(1)} collective-permute-done((f32[3,1,128]{2,1,0:T(1,128)S(1)}, f32[3,1,128]{2,1,0:T(1,128)S(1)}, u32[]{:S(2)}, u32[]{:S(2)}) %collective-permute-start.39) | collective-permute-done | bytes 1568 | tf_op jit(solution)/shard_map/ppermute | solution.py:22
  211.0 3.2 %collective-permute-start.40 = (f32[1,2,128]{2,1,0:T(2,128)S(1)}, f32[1,2,128]{2,1,0:T(2,128)S(1)}, u32[]{:S(2)}, u32[]{:S(2)}) collective-permute-start(f32[1,2,128]{2,1,0:T(2,128)S(1)} %divide_add_fusion.1), channel_id=1, source_target_pairs={{0,4},{4,8},{8,12},{12,16},{16,20},{20,24},{24,28},{1,5},{5,9},{9,... | collective-permute-start | bytes 3080 | tf_op jit(solution)/shard_map/ppermute | solution.py:20
  215.5 3.2 %collective-permute-done.41 = f32[1,2,128]{2,1,0:T(2,128)S(1)} collective-permute-done((f32[1,2,128]{2,1,0:T(2,128)S(1)}, f32[1,2,128]{2,1,0:T(2,128)S(1)}, u32[]{:S(2)}, u32[]{:S(2)}) %collective-permute-start.41) | collective-permute-done | bytes 1056 | tf_op jit(solution)/shard_map/ppermute | solution.py:22
  222.0 4.2 %collective-permute-done.43 = f32[3,1,128]{2,1,0:T(1,128)S(1)} collective-permute-done((f32[3,1,128]{2,1,0:T(1,128)S(1)}, f32[3,1,128]{2,1,0:T(1,128)S(1)}, u32[]{:S(2)}, u32[]{:S(2)}) %collective-permute-start.43) | collective-permute-done | bytes 1568 | tf_op jit(solution)/shard_map/ppermute | solution.py:22
  226.3 3.2 %collective-permute-start.44 = (f32[1,2,128]{2,1,0:T(2,128)S(1)}, f32[1,2,128]{2,1,0:T(2,128)S(1)}, u32[]{:S(2)}, u32[]{:S(2)}) collective-permute-start(f32[1,2,128]{2,1,0:T(2,128)S(1)} %divide_add_fusion), channel_id=1, source_target_pairs={{0,4},{4,8},{8,12},{12,16},{16,20},{20,24},{24,28},{1,5},{5,9},{9,... | collective-permute-start | bytes 3080 | tf_op jit(solution)/shard_map/ppermute | solution.py:20
  230.8 3.2 %collective-permute-done.45 = f32[1,2,128]{2,1,0:T(2,128)S(1)} collective-permute-done((f32[1,2,128]{2,1,0:T(2,128)S(1)}, f32[1,2,128]{2,1,0:T(2,128)S(1)}, u32[]{:S(2)}, u32[]{:S(2)}) %collective-permute-start.45) | collective-permute-done | bytes 1056 | tf_op jit(solution)/shard_map/ppermute | solution.py:22
  237.3 4.2 %collective-permute-done.47 = f32[3,1,128]{2,1,0:T(1,128)S(1)} collective-permute-done((f32[3,1,128]{2,1,0:T(1,128)S(1)}, f32[3,1,128]{2,1,0:T(1,128)S(1)}, u32[]{:S(2)}, u32[]{:S(2)}) %collective-permute-start.47) | collective-permute-done | bytes 1568 | tf_op jit(solution)/shard_map/ppermute | solution.py:22
  242.0 3.2 %collective-permute-start.48 = (f32[1,4,256]{2,1,0:T(4,128)S(1)}, f32[1,4,256]{2,1,0:T(4,128)S(1)}, u32[]{:S(2)}, u32[]{:S(2)}) collective-permute-start(f32[1,4,256]{2,1,0:T(4,128)S(1)} %get-tuple-element.34), channel_id=1, source_target_pairs={{0,4},{4,8},{8,12},{12,16},{16,20},{20,24},{24,28},{1,5},{5,9},{9,... | collective-permute-start | bytes 12296 | tf_op jit(solution)/shard_map/ppermute | solution.py:20
  246.5 3.3 %collective-permute-done.49 = f32[1,4,256]{2,1,0:T(4,128)S(1)} collective-permute-done((f32[1,4,256]{2,1,0:T(4,128)S(1)}, f32[1,4,256]{2,1,0:T(4,128)S(1)}, u32[]{:S(2)}, u32[]{:S(2)}) %collective-permute-start.49) | collective-permute-done | bytes 4128 | tf_op jit(solution)/shard_map/ppermute | solution.py:22
  249.8 1.9 collective-permute-start.50
  253.0 4.2 %collective-permute-done.51 = f32[4,1,256]{2,1,0:T(1,128)S(1)} collective-permute-done((f32[4,1,256]{2,1,0:T(1,128)S(1)}, f32[4,1,256]{2,1,0:T(1,128)S(1)}, u32[]{:S(2)}, u32[]{:S(2)}) %collective-permute-start.51) | collective-permute-done | bytes 4128 | tf_op jit(solution)/shard_map/ppermute | solution.py:22
  257.4 2.5 broadcast_in_dim.50
  259.9 4.0 %reshape.182 = f32[4,8,512]{2,1,0:T(8,128)S(1)} reshape(f32[2,2,4,2,256,2]{5,4,3,2,1,0:T(8,128)} %broadcast_in_dim.50) | data formatting | bytes 131072 | tf_op jit(solution)/shard_map/reshape | solution.py:93
  264.0 3.2 %collective-permute-start.52 = (f32[1,8,512]{2,1,0:T(8,128)S(1)}, f32[1,8,512]{2,1,0:T(8,128)S(1)}, u32[]{:S(2)}, u32[]{:S(2)}) collective-permute-start(f32[1,8,512]{2,1,0:T(8,128)S(1)} %get-tuple-element.20), channel_id=1, source_target_pairs={{0,4},{4,8},{8,12},{12,16},{16,20},{20,24},{24,28},{1,5},{5,9},{9,... | collective-permute-start | bytes 49160 | tf_op jit(solution)/shard_map/ppermute | solution.py:20
  268.5 3.3 %collective-permute-done.53 = f32[1,8,512]{2,1,0:T(8,128)S(1)} collective-permute-done((f32[1,8,512]{2,1,0:T(8,128)S(1)}, f32[1,8,512]{2,1,0:T(8,128)S(1)}, u32[]{:S(2)}, u32[]{:S(2)}) %collective-permute-start.53) | collective-permute-done | bytes 16416 | tf_op jit(solution)/shard_map/ppermute | solution.py:22
  271.8 1.9 collective-permute-start.54
  275.1 4.2 %collective-permute-done.55 = f32[6,1,512]{2,1,0:T(1,128)S(1)} collective-permute-done((f32[6,1,512]{2,1,0:T(1,128)S(1)}, f32[6,1,512]{2,1,0:T(1,128)S(1)}, u32[]{:S(2)}, u32[]{:S(2)}) %collective-permute-start.55) | collective-permute-done | bytes 12320 | tf_op jit(solution)/shard_map/ppermute | solution.py:22
  (149 shorter events, 54.8 us)
Async XLA Ops:
  4.2 3.7 %collective-permute-start = (f32[1,8,512]{2,1,0:T(8,128)S(1)}, f32[1,8,512]{2,1,0:T(8,128)S(1)}, u32[]{:S(2)}, u32[]{:S(2)}) collective-permute-start(f32[1,8,512]{2,1,0:T(8,128)S(1)} %get-tuple-element.26), channel_id=1, source_target_pairs={{0,4},{4,8},{8,12},{12,16},{16,20},{20,24},{24,28},{1,5},{5,9},{9,... | collective-permute-start | bytes 49160 | tf_op jit(solution)/shard_map/ppermute | solution.py:20
  6.5 5.2 %collective-permute-start.1 = (f32[1,8,512]{2,1,0:T(8,128)S(1)}, f32[1,8,512]{2,1,0:T(8,128)S(1)}, u32[]{:S(2)}, u32[]{:S(2)}) collective-permute-start(f32[1,8,512]{2,1,0:T(8,128)S(1)} %get-tuple-element.27), channel_id=1, source_target_pairs={{4,0},{8,4},{12,8},{16,12},{20,16},{24,20},{28,24},{5,1},{9,5},{13... | collective-permute-start | bytes 49160 | tf_op jit(solution)/shard_map/ppermute | solution.py:22
  11.7 4.9 %collective-permute-start.2 = (f32[6,1,512]{2,1,0:T(1,128)S(1)}, f32[6,1,512]{2,1,0:T(1,128)S(1)}, u32[]{:S(2)}, u32[]{:S(2)}) collective-permute-start(f32[6,1,512]{2,1,0:T(1,128)S(1)} %get-tuple-element.18), channel_id=1, source_target_pairs={{0,1},{1,2},{2,3},{4,5},{5,6},{6,7},{8,9},{9,10},{10,11},{12,13},{... | collective-permute-start | bytes 36872 | tf_op jit(solution)/shard_map/ppermute | solution.py:20
  15.2 5.6 %collective-permute-start.3 = (f32[6,1,512]{2,1,0:T(1,128)S(1)}, f32[6,1,512]{2,1,0:T(1,128)S(1)}, u32[]{:S(2)}, u32[]{:S(2)}) collective-permute-start(f32[6,1,512]{2,1,0:T(1,128)S(1)} %get-tuple-element.19), channel_id=1, source_target_pairs={{1,0},{2,1},{3,2},{5,4},{6,5},{7,6},{9,8},{10,9},{11,10},{13,12},{... | collective-permute-start | bytes 36872 | tf_op jit(solution)/shard_map/ppermute | solution.py:22
  44.3 22.2 %collective-permute-start.4 = (f32[1,8,512]{2,1,0:T(8,128)S(1)}, f32[1,8,512]{2,1,0:T(8,128)S(1)}, u32[]{:S(2)}, u32[]{:S(2)}) collective-permute-start(f32[1,8,512]{2,1,0:T(8,128)S(1)} %get-tuple-element.24), channel_id=1, source_target_pairs={{0,4},{4,8},{8,12},{12,16},{16,20},{20,24},{24,28},{1,5},{5,9},{9,... | collective-permute-start | bytes 49160 | tf_op jit(solution)/shard_map/ppermute | solution.py:20
  47.2 7.5 %copy-start = (f32[2,2,4,2,256,2]{5,4,3,2,1,0:T(8,128)S(1)}, f32[2,2,4,2,256,2]{5,4,3,2,1,0:T(8,128)}, u32[]{:S(2)}) copy-start(f32[2,2,4,2,256,2]{5,4,3,2,1,0:T(8,128)} %squeeze.62) | copy-start | bytes 196612
  47.2 7.5 %copy-start.1 = (f32[2,2,4,2,256,2]{5,4,3,2,1,0:T(8,128)S(1)}, f32[2,2,4,2,256,2]{5,4,3,2,1,0:T(8,128)}, u32[]{:S(2)}) copy-start(f32[2,2,4,2,256,2]{5,4,3,2,1,0:T(8,128)} %squeeze.63) | copy-start | bytes 196612
  47.3 19.2 %collective-permute-start.5 = (f32[1,8,512]{2,1,0:T(8,128)S(1)}, f32[1,8,512]{2,1,0:T(8,128)S(1)}, u32[]{:S(2)}, u32[]{:S(2)}) collective-permute-start(f32[1,8,512]{2,1,0:T(8,128)S(1)} %get-tuple-element.25), channel_id=1, source_target_pairs={{4,0},{8,4},{12,8},{16,12},{20,16},{24,20},{28,24},{5,1},{9,5},{13... | collective-permute-start | bytes 49160 | tf_op jit(solution)/shard_map/ppermute | solution.py:22
  61.0 14.8 %copy-start.2 = (f32[4,8,512]{2,1,0:T(8,128)S(1)}, f32[4,8,512]{2,1,0:T(8,128)}, u32[]{:S(2)}) copy-start(f32[4,8,512]{2,1,0:T(8,128)} %param.3) | copy-start | bytes 196612
  66.5 8.1 %collective-permute-start.6 = (f32[6,1,512]{2,1,0:T(1,128)S(1)}, f32[6,1,512]{2,1,0:T(1,128)S(1)}, u32[]{:S(2)}, u32[]{:S(2)}) collective-permute-start(f32[6,1,512]{2,1,0:T(1,128)S(1)} %get-tuple-element.16), channel_id=1, source_target_pairs={{0,1},{1,2},{2,3},{4,5},{5,6},{6,7},{8,9},{9,10},{10,11},{12,13},{... | collective-permute-start | bytes 36872 | tf_op jit(solution)/shard_map/ppermute | solution.py:20
  70.0 5.6 %collective-permute-start.7 = (f32[6,1,512]{2,1,0:T(1,128)S(1)}, f32[6,1,512]{2,1,0:T(1,128)S(1)}, u32[]{:S(2)}, u32[]{:S(2)}) collective-permute-start(f32[6,1,512]{2,1,0:T(1,128)S(1)} %get-tuple-element.17), channel_id=1, source_target_pairs={{1,0},{2,1},{3,2},{5,4},{6,5},{7,6},{9,8},{10,9},{11,10},{13,12},{... | collective-permute-start | bytes 36872 | tf_op jit(solution)/shard_map/ppermute | solution.py:22
  75.9 4.6 %collective-permute-start.8 = (f32[1,8,512]{2,1,0:T(8,128)S(1)}, f32[1,8,512]{2,1,0:T(8,128)S(1)}, u32[]{:S(2)}, u32[]{:S(2)}) collective-permute-start(f32[1,8,512]{2,1,0:T(8,128)S(1)} %get-tuple-element.22), channel_id=1, source_target_pairs={{0,4},{4,8},{8,12},{12,16},{16,20},{20,24},{24,28},{1,5},{5,9},{9,... | collective-permute-start | bytes 49160 | tf_op jit(solution)/shard_map/ppermute | solution.py:20
  78.2 5.4 %collective-permute-start.9 = (f32[1,8,512]{2,1,0:T(8,128)S(1)}, f32[1,8,512]{2,1,0:T(8,128)S(1)}, u32[]{:S(2)}, u32[]{:S(2)}) collective-permute-start(f32[1,8,512]{2,1,0:T(8,128)S(1)} %get-tuple-element.23), channel_id=1, source_target_pairs={{4,0},{8,4},{12,8},{16,12},{20,16},{24,20},{28,24},{5,1},{9,5},{13... | collective-permute-start | bytes 49160 | tf_op jit(solution)/shard_map/ppermute | solution.py:22
  83.7 5.5 %collective-permute-start.10 = (f32[6,1,512]{2,1,0:T(1,128)S(1)}, f32[6,1,512]{2,1,0:T(1,128)S(1)}, u32[]{:S(2)}, u32[]{:S(2)}) collective-permute-start(f32[6,1,512]{2,1,0:T(1,128)S(1)} %get-tuple-element.14), channel_id=1, source_target_pairs={{0,1},{1,2},{2,3},{4,5},{5,6},{6,7},{8,9},{9,10},{10,11},{12,13},{... | collective-permute-start | bytes 36872 | tf_op jit(solution)/shard_map/ppermute | solution.py:20
  87.3 5.6 %collective-permute-start.11 = (f32[6,1,512]{2,1,0:T(1,128)S(1)}, f32[6,1,512]{2,1,0:T(1,128)S(1)}, u32[]{:S(2)}, u32[]{:S(2)}) collective-permute-start(f32[6,1,512]{2,1,0:T(1,128)S(1)} %get-tuple-element.15), channel_id=1, source_target_pairs={{1,0},{2,1},{3,2},{5,4},{6,5},{7,6},{9,8},{10,9},{11,10},{13,12},{... | collective-permute-start | bytes 36872 | tf_op jit(solution)/shard_map/ppermute | solution.py:22
  101.4 4.9 %collective-permute-start.12 = (f32[1,4,256]{2,1,0:T(4,128)S(1)}, f32[1,4,256]{2,1,0:T(4,128)S(1)}, u32[]{:S(2)}, u32[]{:S(2)}) collective-permute-start(f32[1,4,256]{2,1,0:T(4,128)S(1)} %get-tuple-element.38), channel_id=1, source_target_pairs={{0,4},{4,8},{8,12},{12,16},{16,20},{20,24},{24,28},{1,5},{5,9},{9,... | collective-permute-start | bytes 12296 | tf_op jit(solution)/shard_map/ppermute | solution.py:20
  104.4 4.8 %collective-permute-start.13 = (f32[1,4,256]{2,1,0:T(4,128)S(1)}, f32[1,4,256]{2,1,0:T(4,128)S(1)}, u32[]{:S(2)}, u32[]{:S(2)}) collective-permute-start(f32[1,4,256]{2,1,0:T(4,128)S(1)} %get-tuple-element.39), channel_id=1, source_target_pairs={{4,0},{8,4},{12,8},{16,12},{20,16},{24,20},{28,24},{5,1},{9,5},{13... | collective-permute-start | bytes 12296 | tf_op jit(solution)/shard_map/ppermute | solution.py:22
  109.2 5.4 %collective-permute-start.14 = (f32[4,1,256]{2,1,0:T(1,128)S(1)}, f32[4,1,256]{2,1,0:T(1,128)S(1)}, u32[]{:S(2)}, u32[]{:S(2)}) collective-permute-start(f32[4,1,256]{2,1,0:T(1,128)S(1)} %get-tuple-element.32), channel_id=1, source_target_pairs={{0,1},{1,2},{2,3},{4,5},{5,6},{6,7},{8,9},{9,10},{10,11},{12,13},{... | collective-permute-start | bytes 12296 | tf_op jit(solution)/shard_map/ppermute | solution.py:20
  112.7 5.5 %collective-permute-start.15 = (f32[4,1,256]{2,1,0:T(1,128)S(1)}, f32[4,1,256]{2,1,0:T(1,128)S(1)}, u32[]{:S(2)}, u32[]{:S(2)}) collective-permute-start(f32[4,1,256]{2,1,0:T(1,128)S(1)} %get-tuple-element.33), channel_id=1, source_target_pairs={{1,0},{2,1},{3,2},{5,4},{6,5},{7,6},{9,8},{10,9},{11,10},{13,12},{... | collective-permute-start | bytes 12296 | tf_op jit(solution)/shard_map/ppermute | solution.py:22
  118.4 5.0 %collective-permute-start.16 = (f32[1,4,256]{2,1,0:T(4,128)S(1)}, f32[1,4,256]{2,1,0:T(4,128)S(1)}, u32[]{:S(2)}, u32[]{:S(2)}) collective-permute-start(f32[1,4,256]{2,1,0:T(4,128)S(1)} %get-tuple-element.36), channel_id=1, source_target_pairs={{0,4},{4,8},{8,12},{12,16},{16,20},{20,24},{24,28},{1,5},{5,9},{9,... | collective-permute-start | bytes 12296 | tf_op jit(solution)/shard_map/ppermute | solution.py:20
  121.4 4.8 %collective-permute-start.17 = (f32[1,4,256]{2,1,0:T(4,128)S(1)}, f32[1,4,256]{2,1,0:T(4,128)S(1)}, u32[]{:S(2)}, u32[]{:S(2)}) collective-permute-start(f32[1,4,256]{2,1,0:T(4,128)S(1)} %get-tuple-element.37), channel_id=1, source_target_pairs={{4,0},{8,4},{12,8},{16,12},{20,16},{24,20},{28,24},{5,1},{9,5},{13... | collective-permute-start | bytes 12296 | tf_op jit(solution)/shard_map/ppermute | solution.py:22
  126.3 3.3 %collective-permute-start.18 = (f32[4,1,256]{2,1,0:T(1,128)S(1)}, f32[4,1,256]{2,1,0:T(1,128)S(1)}, u32[]{:S(2)}, u32[]{:S(2)}) collective-permute-start(f32[4,1,256]{2,1,0:T(1,128)S(1)} %get-tuple-element.30), channel_id=1, source_target_pairs={{0,1},{1,2},{2,3},{4,5},{5,6},{6,7},{8,9},{9,10},{10,11},{12,13},{... | collective-permute-start | bytes 12296 | tf_op jit(solution)/shard_map/ppermute | solution.py:20
  128.2 5.5 %collective-permute-start.19 = (f32[4,1,256]{2,1,0:T(1,128)S(1)}, f32[4,1,256]{2,1,0:T(1,128)S(1)}, u32[]{:S(2)}, u32[]{:S(2)}) collective-permute-start(f32[4,1,256]{2,1,0:T(1,128)S(1)} %get-tuple-element.31), channel_id=1, source_target_pairs={{1,0},{2,1},{3,2},{5,4},{6,5},{7,6},{9,8},{10,9},{11,10},{13,12},{... | collective-permute-start | bytes 12296 | tf_op jit(solution)/shard_map/ppermute | solution.py:22
  134.3 4.5 %collective-permute-start.20 = (f32[1,2,128]{2,1,0:T(2,128)S(1)}, f32[1,2,128]{2,1,0:T(2,128)S(1)}, u32[]{:S(2)}, u32[]{:S(2)}) collective-permute-start(f32[1,2,128]{2,1,0:T(2,128)S(1)} %fusion.206), channel_id=1, source_target_pairs={{0,4},{4,8},{8,12},{12,16},{16,20},{20,24},{24,28},{1,5},{5,9},{9,... | collective-permute-start | bytes 3080 | tf_op jit(solution)/shard_map/ppermute | solution.py:20
  137.5 4.5 %collective-permute-start.21 = (f32[1,2,128]{2,1,0:T(2,128)S(1)}, f32[1,2,128]{2,1,0:T(2,128)S(1)}, u32[]{:S(2)}, u32[]{:S(2)}) collective-permute-start(f32[1,2,128]{2,1,0:T(2,128)S(1)} %fusion.206), channel_id=1, source_target_pairs={{4,0},{8,4},{12,8},{16,12},{20,16},{24,20},{28,24},{5,1},{9,5},{13... | collective-permute-start | bytes 3080 | tf_op jit(solution)/shard_map/ppermute | solution.py:22
  142.1 3.2 %collective-permute-start.22 = (f32[3,1,128]{2,1,0:T(1,128)S(1)}, f32[3,1,128]{2,1,0:T(1,128)S(1)}, u32[]{:S(2)}, u32[]{:S(2)}) collective-permute-start(f32[3,1,128]{2,1,0:T(1,128)S(1)} %get-tuple-element.52), channel_id=1, source_target_pairs={{0,1},{1,2},{2,3},{4,5},{5,6},{6,7},{8,9},{9,10},{10,11},{12,13},{... | collective-permute-start | bytes 4616 | tf_op jit(solution)/shard_map/ppermute | solution.py:20
  144.0 5.5 %collective-permute-start.23 = (f32[3,1,128]{2,1,0:T(1,128)S(1)}, f32[3,1,128]{2,1,0:T(1,128)S(1)}, u32[]{:S(2)}, u32[]{:S(2)}) collective-permute-start(f32[3,1,128]{2,1,0:T(1,128)S(1)} %get-tuple-element.53), channel_id=1, source_target_pairs={{1,0},{2,1},{3,2},{5,4},{6,5},{7,6},{9,8},{10,9},{11,10},{13,12},{... | collective-permute-start | bytes 4616 | tf_op jit(solution)/shard_map/ppermute | solution.py:22
  149.7 4.5 %collective-permute-start.24 = (f32[1,2,128]{2,1,0:T(2,128)S(1)}, f32[1,2,128]{2,1,0:T(2,128)S(1)}, u32[]{:S(2)}, u32[]{:S(2)}) collective-permute-start(f32[1,2,128]{2,1,0:T(2,128)S(1)} %divide_add_fusion.5), channel_id=1, source_target_pairs={{0,4},{4,8},{8,12},{12,16},{16,20},{20,24},{24,28},{1,5},{5,9},{9,... | collective-permute-start | bytes 3080 | tf_op jit(solution)/shard_map/ppermute | solution.py:20
  152.9 4.5 %collective-permute-start.25 = (f32[1,2,128]{2,1,0:T(2,128)S(1)}, f32[1,2,128]{2,1,0:T(2,128)S(1)}, u32[]{:S(2)}, u32[]{:S(2)}) collective-permute-start(f32[1,2,128]{2,1,0:T(2,128)S(1)} %divide_add_fusion.5), channel_id=1, source_target_pairs={{4,0},{8,4},{12,8},{16,12},{20,16},{24,20},{28,24},{5,1},{9,5},{13... | collective-permute-start | bytes 3080 | tf_op jit(solution)/shard_map/ppermute | solution.py:22
  157.4 3.2 %collective-permute-start.26 = (f32[3,1,128]{2,1,0:T(1,128)S(1)}, f32[3,1,128]{2,1,0:T(1,128)S(1)}, u32[]{:S(2)}, u32[]{:S(2)}) collective-permute-start(f32[3,1,128]{2,1,0:T(1,128)S(1)} %get-tuple-element.50), channel_id=1, source_target_pairs={{0,1},{1,2},{2,3},{4,5},{5,6},{6,7},{8,9},{9,10},{10,11},{12,13},{... | collective-permute-start | bytes 4616 | tf_op jit(solution)/shard_map/ppermute | solution.py:20
  159.3 5.5 %collective-permute-start.27 = (f32[3,1,128]{2,1,0:T(1,128)S(1)}, f32[3,1,128]{2,1,0:T(1,128)S(1)}, u32[]{:S(2)}, u32[]{:S(2)}) collective-permute-start(f32[3,1,128]{2,1,0:T(1,128)S(1)} %get-tuple-element.51), channel_id=1, source_target_pairs={{1,0},{2,1},{3,2},{5,4},{6,5},{7,6},{9,8},{10,9},{11,10},{13,12},{... | collective-permute-start | bytes 4616 | tf_op jit(solution)/shard_map/ppermute | solution.py:22
  165.0 4.5 %collective-permute-start.28 = (f32[1,2,128]{2,1,0:T(2,128)S(1)}, f32[1,2,128]{2,1,0:T(2,128)S(1)}, u32[]{:S(2)}, u32[]{:S(2)}) collective-permute-start(f32[1,2,128]{2,1,0:T(2,128)S(1)} %divide_add_fusion.4), channel_id=1, source_target_pairs={{0,4},{4,8},{8,12},{12,16},{16,20},{20,24},{24,28},{1,5},{5,9},{9,... | collective-permute-start | bytes 3080 | tf_op jit(solution)/shard_map/ppermute | solution.py:20
  168.2 4.6 %collective-permute-start.29 = (f32[1,2,128]{2,1,0:T(2,128)S(1)}, f32[1,2,128]{2,1,0:T(2,128)S(1)}, u32[]{:S(2)}, u32[]{:S(2)}) collective-permute-start(f32[1,2,128]{2,1,0:T(2,128)S(1)} %divide_add_fusion.4), channel_id=1, source_target_pairs={{4,0},{8,4},{12,8},{16,12},{20,16},{24,20},{28,24},{5,1},{9,5},{13... | collective-permute-start | bytes 3080 | tf_op jit(solution)/shard_map/ppermute | solution.py:22
  172.7 3.2 %collective-permute-start.30 = (f32[3,1,128]{2,1,0:T(1,128)S(1)}, f32[3,1,128]{2,1,0:T(1,128)S(1)}, u32[]{:S(2)}, u32[]{:S(2)}) collective-permute-start(f32[3,1,128]{2,1,0:T(1,128)S(1)} %get-tuple-element.48), channel_id=1, source_target_pairs={{0,1},{1,2},{2,3},{4,5},{5,6},{6,7},{8,9},{9,10},{10,11},{12,13},{... | collective-permute-start | bytes 4616 | tf_op jit(solution)/shard_map/ppermute | solution.py:20
  174.7 5.5 %collective-permute-start.31 = (f32[3,1,128]{2,1,0:T(1,128)S(1)}, f32[3,1,128]{2,1,0:T(1,128)S(1)}, u32[]{:S(2)}, u32[]{:S(2)}) collective-permute-start(f32[3,1,128]{2,1,0:T(1,128)S(1)} %get-tuple-element.49), channel_id=1, source_target_pairs={{1,0},{2,1},{3,2},{5,4},{6,5},{7,6},{9,8},{10,9},{11,10},{13,12},{... | collective-permute-start | bytes 4616 | tf_op jit(solution)/shard_map/ppermute | solution.py:22
  180.3 4.5 %collective-permute-start.32 = (f32[1,2,128]{2,1,0:T(2,128)S(1)}, f32[1,2,128]{2,1,0:T(2,128)S(1)}, u32[]{:S(2)}, u32[]{:S(2)}) collective-permute-start(f32[1,2,128]{2,1,0:T(2,128)S(1)} %divide_add_fusion.3), channel_id=1, source_target_pairs={{0,4},{4,8},{8,12},{12,16},{16,20},{20,24},{24,28},{1,5},{5,9},{9,... | collective-permute-start | bytes 3080 | tf_op jit(solution)/shard_map/ppermute | solution.py:20
  183.5 4.6 %collective-permute-start.33 = (f32[1,2,128]{2,1,0:T(2,128)S(1)}, f32[1,2,128]{2,1,0:T(2,128)S(1)}, u32[]{:S(2)}, u32[]{:S(2)}) collective-permute-start(f32[1,2,128]{2,1,0:T(2,128)S(1)} %divide_add_fusion.3), channel_id=1, source_target_pairs={{4,0},{8,4},{12,8},{16,12},{20,16},{24,20},{28,24},{5,1},{9,5},{13... | collective-permute-start | bytes 3080 | tf_op jit(solution)/shard_map/ppermute | solution.py:22
  188.1 3.2 %collective-permute-start.34 = (f32[3,1,128]{2,1,0:T(1,128)S(1)}, f32[3,1,128]{2,1,0:T(1,128)S(1)}, u32[]{:S(2)}, u32[]{:S(2)}) collective-permute-start(f32[3,1,128]{2,1,0:T(1,128)S(1)} %get-tuple-element.46), channel_id=1, source_target_pairs={{0,1},{1,2},{2,3},{4,5},{5,6},{6,7},{8,9},{9,10},{10,11},{12,13},{... | collective-permute-start | bytes 4616 | tf_op jit(solution)/shard_map/ppermute | solution.py:20
  190.0 5.5 %collective-permute-start.35 = (f32[3,1,128]{2,1,0:T(1,128)S(1)}, f32[3,1,128]{2,1,0:T(1,128)S(1)}, u32[]{:S(2)}, u32[]{:S(2)}) collective-permute-start(f32[3,1,128]{2,1,0:T(1,128)S(1)} %get-tuple-element.47), channel_id=1, source_target_pairs={{1,0},{2,1},{3,2},{5,4},{6,5},{7,6},{9,8},{10,9},{11,10},{13,12},{... | collective-permute-start | bytes 4616 | tf_op jit(solution)/shard_map/ppermute | solution.py:22
  195.7 4.5 %collective-permute-start.36 = (f32[1,2,128]{2,1,0:T(2,128)S(1)}, f32[1,2,128]{2,1,0:T(2,128)S(1)}, u32[]{:S(2)}, u32[]{:S(2)}) collective-permute-start(f32[1,2,128]{2,1,0:T(2,128)S(1)} %divide_add_fusion.2), channel_id=1, source_target_pairs={{0,4},{4,8},{8,12},{12,16},{16,20},{20,24},{24,28},{1,5},{5,9},{9,... | collective-permute-start | bytes 3080 | tf_op jit(solution)/shard_map/ppermute | solution.py:20
  198.8 4.6 %collective-permute-start.37 = (f32[1,2,128]{2,1,0:T(2,128)S(1)}, f32[1,2,128]{2,1,0:T(2,128)S(1)}, u32[]{:S(2)}, u32[]{:S(2)}) collective-permute-start(f32[1,2,128]{2,1,0:T(2,128)S(1)} %divide_add_fusion.2), channel_id=1, source_target_pairs={{4,0},{8,4},{12,8},{16,12},{20,16},{24,20},{28,24},{5,1},{9,5},{13... | collective-permute-start | bytes 3080 | tf_op jit(solution)/shard_map/ppermute | solution.py:22
  203.4 3.2 %collective-permute-start.38 = (f32[3,1,128]{2,1,0:T(1,128)S(1)}, f32[3,1,128]{2,1,0:T(1,128)S(1)}, u32[]{:S(2)}, u32[]{:S(2)}) collective-permute-start(f32[3,1,128]{2,1,0:T(1,128)S(1)} %get-tuple-element.44), channel_id=1, source_target_pairs={{0,1},{1,2},{2,3},{4,5},{5,6},{6,7},{8,9},{9,10},{10,11},{12,13},{... | collective-permute-start | bytes 4616 | tf_op jit(solution)/shard_map/ppermute | solution.py:20
  205.3 5.5 %collective-permute-start.39 = (f32[3,1,128]{2,1,0:T(1,128)S(1)}, f32[3,1,128]{2,1,0:T(1,128)S(1)}, u32[]{:S(2)}, u32[]{:S(2)}) collective-permute-start(f32[3,1,128]{2,1,0:T(1,128)S(1)} %get-tuple-element.45), channel_id=1, source_target_pairs={{1,0},{2,1},{3,2},{5,4},{6,5},{7,6},{9,8},{10,9},{11,10},{13,12},{... | collective-permute-start | bytes 4616 | tf_op jit(solution)/shard_map/ppermute | solution.py:22
  211.0 4.5 %collective-permute-start.40 = (f32[1,2,128]{2,1,0:T(2,128)S(1)}, f32[1,2,128]{2,1,0:T(2,128)S(1)}, u32[]{:S(2)}, u32[]{:S(2)}) collective-permute-start(f32[1,2,128]{2,1,0:T(2,128)S(1)} %divide_add_fusion.1), channel_id=1, source_target_pairs={{0,4},{4,8},{8,12},{12,16},{16,20},{20,24},{24,28},{1,5},{5,9},{9,... | collective-permute-start | bytes 3080 | tf_op jit(solution)/shard_map/ppermute | solution.py:20
  214.2 4.6 %collective-permute-start.41 = (f32[1,2,128]{2,1,0:T(2,128)S(1)}, f32[1,2,128]{2,1,0:T(2,128)S(1)}, u32[]{:S(2)}, u32[]{:S(2)}) collective-permute-start(f32[1,2,128]{2,1,0:T(2,128)S(1)} %divide_add_fusion.1), channel_id=1, source_target_pairs={{4,0},{8,4},{12,8},{16,12},{20,16},{24,20},{28,24},{5,1},{9,5},{13... | collective-permute-start | bytes 3080 | tf_op jit(solution)/shard_map/ppermute | solution.py:22
  218.7 3.2 %collective-permute-start.42 = (f32[3,1,128]{2,1,0:T(1,128)S(1)}, f32[3,1,128]{2,1,0:T(1,128)S(1)}, u32[]{:S(2)}, u32[]{:S(2)}) collective-permute-start(f32[3,1,128]{2,1,0:T(1,128)S(1)} %get-tuple-element.42), channel_id=1, source_target_pairs={{0,1},{1,2},{2,3},{4,5},{5,6},{6,7},{8,9},{9,10},{10,11},{12,13},{... | collective-permute-start | bytes 4616 | tf_op jit(solution)/shard_map/ppermute | solution.py:20
  220.7 5.5 %collective-permute-start.43 = (f32[3,1,128]{2,1,0:T(1,128)S(1)}, f32[3,1,128]{2,1,0:T(1,128)S(1)}, u32[]{:S(2)}, u32[]{:S(2)}) collective-permute-start(f32[3,1,128]{2,1,0:T(1,128)S(1)} %get-tuple-element.43), channel_id=1, source_target_pairs={{1,0},{2,1},{3,2},{5,4},{6,5},{7,6},{9,8},{10,9},{11,10},{13,12},{... | collective-permute-start | bytes 4616 | tf_op jit(solution)/shard_map/ppermute | solution.py:22
  226.3 4.5 %collective-permute-start.44 = (f32[1,2,128]{2,1,0:T(2,128)S(1)}, f32[1,2,128]{2,1,0:T(2,128)S(1)}, u32[]{:S(2)}, u32[]{:S(2)}) collective-permute-start(f32[1,2,128]{2,1,0:T(2,128)S(1)} %divide_add_fusion), channel_id=1, source_target_pairs={{0,4},{4,8},{8,12},{12,16},{16,20},{20,24},{24,28},{1,5},{5,9},{9,... | collective-permute-start | bytes 3080 | tf_op jit(solution)/shard_map/ppermute | solution.py:20
  229.5 4.6 %collective-permute-start.45 = (f32[1,2,128]{2,1,0:T(2,128)S(1)}, f32[1,2,128]{2,1,0:T(2,128)S(1)}, u32[]{:S(2)}, u32[]{:S(2)}) collective-permute-start(f32[1,2,128]{2,1,0:T(2,128)S(1)} %divide_add_fusion), channel_id=1, source_target_pairs={{4,0},{8,4},{12,8},{16,12},{20,16},{24,20},{28,24},{5,1},{9,5},{13... | collective-permute-start | bytes 3080 | tf_op jit(solution)/shard_map/ppermute | solution.py:22
  234.1 3.2 %collective-permute-start.46 = (f32[3,1,128]{2,1,0:T(1,128)S(1)}, f32[3,1,128]{2,1,0:T(1,128)S(1)}, u32[]{:S(2)}, u32[]{:S(2)}) collective-permute-start(f32[3,1,128]{2,1,0:T(1,128)S(1)} %get-tuple-element.40), channel_id=1, source_target_pairs={{0,1},{1,2},{2,3},{4,5},{5,6},{6,7},{8,9},{9,10},{10,11},{12,13},{... | collective-permute-start | bytes 4616 | tf_op jit(solution)/shard_map/ppermute | solution.py:20
  236.0 5.5 %collective-permute-start.47 = (f32[3,1,128]{2,1,0:T(1,128)S(1)}, f32[3,1,128]{2,1,0:T(1,128)S(1)}, u32[]{:S(2)}, u32[]{:S(2)}) collective-permute-start(f32[3,1,128]{2,1,0:T(1,128)S(1)} %get-tuple-element.41), channel_id=1, source_target_pairs={{1,0},{2,1},{3,2},{5,4},{6,5},{7,6},{9,8},{10,9},{11,10},{13,12},{... | collective-permute-start | bytes 4616 | tf_op jit(solution)/shard_map/ppermute | solution.py:22
  242.0 4.5 %collective-permute-start.48 = (f32[1,4,256]{2,1,0:T(4,128)S(1)}, f32[1,4,256]{2,1,0:T(4,128)S(1)}, u32[]{:S(2)}, u32[]{:S(2)}) collective-permute-start(f32[1,4,256]{2,1,0:T(4,128)S(1)} %get-tuple-element.34), channel_id=1, source_target_pairs={{0,4},{4,8},{8,12},{12,16},{16,20},{20,24},{24,28},{1,5},{5,9},{9,... | collective-permute-start | bytes 12296 | tf_op jit(solution)/shard_map/ppermute | solution.py:20
  245.2 4.6 %collective-permute-start.49 = (f32[1,4,256]{2,1,0:T(4,128)S(1)}, f32[1,4,256]{2,1,0:T(4,128)S(1)}, u32[]{:S(2)}, u32[]{:S(2)}) collective-permute-start(f32[1,4,256]{2,1,0:T(4,128)S(1)} %get-tuple-element.35), channel_id=1, source_target_pairs={{4,0},{8,4},{12,8},{16,12},{20,16},{24,20},{28,24},{5,1},{9,5},{13... | collective-permute-start | bytes 12296 | tf_op jit(solution)/shard_map/ppermute | solution.py:22
  249.8 3.2 %collective-permute-start.50 = (f32[4,1,256]{2,1,0:T(1,128)S(1)}, f32[4,1,256]{2,1,0:T(1,128)S(1)}, u32[]{:S(2)}, u32[]{:S(2)}) collective-permute-start(f32[4,1,256]{2,1,0:T(1,128)S(1)} %get-tuple-element.28), channel_id=1, source_target_pairs={{0,1},{1,2},{2,3},{4,5},{5,6},{6,7},{8,9},{9,10},{10,11},{12,13},{... | collective-permute-start | bytes 12296 | tf_op jit(solution)/shard_map/ppermute | solution.py:20
  251.7 5.5 %collective-permute-start.51 = (f32[4,1,256]{2,1,0:T(1,128)S(1)}, f32[4,1,256]{2,1,0:T(1,128)S(1)}, u32[]{:S(2)}, u32[]{:S(2)}) collective-permute-start(f32[4,1,256]{2,1,0:T(1,128)S(1)} %get-tuple-element.29), channel_id=1, source_target_pairs={{1,0},{2,1},{3,2},{5,4},{6,5},{7,6},{9,8},{10,9},{11,10},{13,12},{... | collective-permute-start | bytes 12296 | tf_op jit(solution)/shard_map/ppermute | solution.py:22
  264.0 4.5 %collective-permute-start.52 = (f32[1,8,512]{2,1,0:T(8,128)S(1)}, f32[1,8,512]{2,1,0:T(8,128)S(1)}, u32[]{:S(2)}, u32[]{:S(2)}) collective-permute-start(f32[1,8,512]{2,1,0:T(8,128)S(1)} %get-tuple-element.20), channel_id=1, source_target_pairs={{0,4},{4,8},{8,12},{12,16},{16,20},{20,24},{24,28},{1,5},{5,9},{9,... | collective-permute-start | bytes 49160 | tf_op jit(solution)/shard_map/ppermute | solution.py:20
  267.2 4.6 %collective-permute-start.53 = (f32[1,8,512]{2,1,0:T(8,128)S(1)}, f32[1,8,512]{2,1,0:T(8,128)S(1)}, u32[]{:S(2)}, u32[]{:S(2)}) collective-permute-start(f32[1,8,512]{2,1,0:T(8,128)S(1)} %get-tuple-element.21), channel_id=1, source_target_pairs={{4,0},{8,4},{12,8},{16,12},{20,16},{24,20},{28,24},{5,1},{9,5},{13... | collective-permute-start | bytes 49160 | tf_op jit(solution)/shard_map/ppermute | solution.py:22
  271.8 3.3 %collective-permute-start.54 = (f32[6,1,512]{2,1,0:T(1,128)S(1)}, f32[6,1,512]{2,1,0:T(1,128)S(1)}, u32[]{:S(2)}, u32[]{:S(2)}) collective-permute-start(f32[6,1,512]{2,1,0:T(1,128)S(1)} %get-tuple-element.12), channel_id=1, source_target_pairs={{0,1},{1,2},{2,3},{4,5},{5,6},{6,7},{8,9},{9,10},{10,11},{12,13},{... | collective-permute-start | bytes 36872 | tf_op jit(solution)/shard_map/ppermute | solution.py:20
  273.7 5.6 %collective-permute-start.55 = (f32[6,1,512]{2,1,0:T(1,128)S(1)}, f32[6,1,512]{2,1,0:T(1,128)S(1)}, u32[]{:S(2)}, u32[]{:S(2)}) collective-permute-start(f32[6,1,512]{2,1,0:T(1,128)S(1)} %get-tuple-element.13), channel_id=1, source_target_pairs={{1,0},{2,1},{3,2},{5,4},{6,5},{7,6},{9,8},{10,9},{11,10},{13,12},{... | collective-permute-start | bytes 36872 | tf_op jit(solution)/shard_map/ppermute | solution.py:22
where the time goes:
time: 284 us; the launch traced here: 280 us
  starting transfers between devices  112 us (39%)
  waiting for transfers between devices  96.3 us (34%)
  local copies, waits for them, and re-layouts  50.3 us (18%)
  other arithmetic  20.4 us (7%)
    ppermute x28, waiting for transfers between devices, extended(): lax.ppermute(head, axis, [((i + 1) % count, i) for i in range(ends)])  96.1 us
    ppermute x28, starting transfers between devices, extended(): lax.ppermute(tail, axis, [(i, (i + 1) % count) for i in range(ends)])  75.6 us
    ppermute x28, starting transfers between devices, extended(): lax.ppermute(head, axis, [((i + 1) % count, i) for i in range(ends)])  36.6 us
    reduce_sum x2, other arithmetic, coarsen_couplings(): upper_three = jnp.sum(blocks[5][..., 1], axis=(1, 3))  6.17 us
    squeeze x2, local copies, waits for them, and re-layouts, coarsen_couplings(): lower_one = jnp.sum(blocks[0][:, 0], axis=(2, 4))  6.09 us
    squeeze x2, local copies, waits for them, and re-layouts, coarsen_couplings(): lower_three = jnp.sum(blocks[4][..., 0], axis=(1, 3))  6.09 us
    squeeze x2, local copies, waits for them, and re-layouts, coarsen_couplings(): upper_two = jnp.sum(blocks[3][:, :, :, 1], axis=(1, 4))  6.05 us
    squeeze x2, local copies, waits for them, and re-layouts, coarsen_couplings(): upper_one = jnp.sum(blocks[1][:, 1], axis=(2, 4))  6 us
  transfers between devices with their start and end apart: 56, of which 29 were waited for; matrix products, arithmetic and copies ran while one was open for 9% of the time, Pallas kernels for 0%

commit v1 on v0

v1 whole, which is shorter than its diff:
```python
import functools

import jax
import jax.numpy as jnp
from jax import lax
from jax.experimental import pallas as pl
from jax.experimental.pallas import tpu as pltpu
from jax.sharding import PartitionSpec as P

SWEEPS = 8
OMEGA = 0.8
KEEP = 1.0 - OMEGA
MESH = pl.DeviceIdType.MESH
TINY = 1e-30

DIRECTIONS = ((1, 0), (-1, 0), (0, 1), (0, -1), (1, 1), (1, -1), (-1, 1), (-1, -1))

ROW0 = 4


def span(step, width, count, first):
    if step == 0:
        return first, first, count
    if step > 0:
        return first + count - width, first - width, width
    return first, first + count, width


def shift(v, by, axis):
    return pltpu.roll(v, by % v.shape[axis], axis)


def flow(low, high, hy, hz, v_low, v, v_high, s):
    a, b = v.ndim - 2, v.ndim - 1
    total = low * v_low + high * v_high
    total = total + hy * shift(v, -s, a) + shift(hy * v, s, a)
    return total + hz * shift(v, -s, b) + shift(hz * v, s, b)


def exact_dot(a, b):
    return jnp.dot(a, b, preferred_element_type=jnp.float32, precision=lax.Precision.HIGHEST)


def kernel(gx, gy, nx, ny, rhs_ref, lab_ref, tab_ref, out_ref, K, R, V1, V2, CC, CB, CR, own_cc, own_cb,
           bytes_cc, bytes_cb, send, recv, g_send, g_recv):
    i = lax.axis_index("gx")
    j = lax.axis_index("gy")
    n = gx * gy
    me = i * gy + j
    nz = rhs_ref.shape[2]
    mx = nx // 2
    tile = (2 * ROW0 + ny, nz)

    for buf in (K, R, V1, V2):
        buf[...] = jnp.zeros(buf.shape, jnp.float32)

    def other(k):
        t = lax.rem(me + k, n)
        return (t // gy, lax.rem(t, gy))

    barrier = pltpu.get_barrier_semaphore()

    def greet(k, c):
        pl.semaphore_signal(barrier, inc=1, device_id=other(k), device_id_type=MESH)
        return c

    lax.fori_loop(1, n, greet, 0)
    rows = slice(ROW0, ROW0 + ny)
    t0, t1, t2 = tab_ref[0], tab_ref[1], tab_ref[2]
    labels = lab_ref[...]
    K[3:3 + nx, rows, :] = jnp.where(labels == 0, t0, jnp.where(labels == 1, t1, t2))
    R[2:2 + nx, rows, :] = rhs_ref[...]
    pl.semaphore_wait(barrier, n - 1)

    def there(dx, dy):
        ok = None
        for at, d, size in ((i, dx, gx), (j, dy, gy)):
            if d:
                c = (at < size - 1) if d > 0 else (at > 0)
                ok = c if ok is None else jnp.logical_and(ok, c)
        return ok

    def halo_copy(buf, which, d, x0, cx, y0, cy, wx, wy, corner_x, corner_y):
        dx, dy = DIRECTIONS[d]
        both = dx != 0 and dy != 0
        sx, tx, lx = span(dx, corner_x if both else wx, cx, x0)
        sy, ty, ly = span(dy, corner_y if both else wy, cy, y0)
        return pltpu.make_async_remote_copy(
            src_ref=buf.at[sx:sx + lx, sy:sy + ly, :],
            dst_ref=buf.at[tx:tx + lx, ty:ty + ly, :],
            send_sem=send.at[which, d],
            recv_sem=recv.at[which, d],
            device_id=(i + dx, j + dy),
            device_id_type=MESH,
        )

    halos = {
        0: (K, 3, nx, ROW0, ny, 3, 3, 2, 2),
        1: (R, 2, nx, ROW0, ny, 2, 2, 1, 1),
        2: (V1, 2, mx, ROW0, ny, 2, 4, 1, 2),
        3: (V2, 2, mx, ROW0, ny, 2, 4, 1, 2),
    }

    def each(which, what):
        for d, (dx, dy) in enumerate(DIRECTIONS):
            sign = -1 if what == "wait_recv" else 1

            @pl.when(there(sign * dx, sign * dy))
            def _():
                buf, *sizes = halos[which]
                getattr(halo_copy(buf, which, d, *sizes), what)()

    each(0, "start")
    each(1, "start")

    row = lax.broadcasted_iota(jnp.int32, tile, 0)
    lane = lax.broadcasted_iota(jnp.int32, tile, 1)
    odd_row = (row & 1) == 1
    odd_lane = (lane & 1) == 1
    last_lane = lane == nz - 1
    first_lane = lane == 0

    def pair(v, axis):
        odd = odd_row if axis == 0 else odd_lane
        return v + jnp.where(odd, shift(v, 1, axis), shift(v, -1, axis))

    def upper(v, axis):
        odd = odd_row if axis == 0 else odd_lane
        return jnp.where(odd, v, shift(v, -1, axis))

    each(0, "wait_recv")
    nk = nx + 6
    k = [K[x] for x in range(nk)]

    def harmonic(a, b):
        return 2.0 * (a * b) / jnp.maximum(a + b, TINY)

    hx = [harmonic(k[x], k[x + 1]) for x in range(nk - 1)]
    hy, hz, edge, diag, inv = ([None] * nk for _ in range(5))
    for x in range(1, nk - 1):
        a = k[x]
        y_up, y_low = shift(a, -1, 0), shift(a, 1, 0)
        z_up = jnp.where(last_lane, 0.0, shift(a, -1, 1))
        hy[x] = harmonic(a, y_up)
        hz[x] = harmonic(a, z_up)
        beyond = jnp.where(k[x - 1] > 0.0, 0.0, a) + jnp.where(k[x + 1] > 0.0, 0.0, a)
        beyond = beyond + jnp.where(y_up > 0.0, 0.0, a) + jnp.where(y_low > 0.0, 0.0, a)
        edge[x] = beyond + jnp.where(first_lane, a, 0.0) + jnp.where(last_lane, a, 0.0)
        diag[x] = (hx[x - 1] + hx[x]) + (hy[x] + shift(hy[x], 1, 0)) + (hz[x] + shift(hz[x], 1, 1)) + edge[x]
        inv[x] = OMEGA / jnp.maximum(diag[x], TINY)

    nm = mx + 4
    gxu = [None] * nm
    gyu, gzu, medge, mdiag, minv = ([None] * nm for _ in range(5))
    for m in range(nm - 1):
        gxu[m] = pair(pair(hx[2 * m], 0), 1)
    for m in range(1, nm - 1):
        x = 2 * m - 1
        gyu[m] = upper(pair(hy[x] + hy[x + 1], 1), 0)
        gzu[m] = upper(pair(hz[x] + hz[x + 1], 0), 1)
        medge[m] = pair(pair(edge[x] + edge[x + 1], 0), 1)
        mdiag[m] = (gxu[m - 1] + gxu[m]) + (gyu[m] + shift(gyu[m], 2, 0))
        mdiag[m] = mdiag[m] + (gzu[m] + shift(gzu[m], 2, 1)) + medge[m]
        minv[m] = OMEGA / jnp.maximum(mdiag[m], TINY)

    each(1, "wait_recv")
    u1, u2 = [None] * nk, [None] * nk
    for x in range(1, nk - 1):
        u1[x] = R[x - 1] * inv[x]
    for x in range(2, nk - 2):
        around = flow(hx[x - 1], hx[x], hy[x], hz[x], u1[x - 1], u1[x], u1[x + 1], 1)
        u2[x] = (1.0 + KEEP) * u1[x] + inv[x] * around
    res = [None] * nk
    for x in range(3, nk - 3):
        around = flow(hx[x - 1], hx[x], hy[x], hz[x], u2[x - 1], u2[x], u2[x + 1], 1)
        res[x] = diag[x] * (u1[x] * (1.0 / OMEGA) - u2[x]) + around

    for m in range(2, nm - 2):
        x = 2 * m - 1
        source = pair(pair(res[x] + res[x + 1], 0), 1)
        V1[m, rows, :] = (source * minv[m])[rows]
    each(2, "start")

    def cells(v):
        return jnp.concatenate([v[0:1] + v[2:3], v[4:5] + v[6:7]], axis=0)

    z = lax.broadcasted_iota(jnp.int32, (nz, nz // 4), 0)
    q = lax.broadcasted_iota(jnp.int32, (nz, nz // 4), 1)
    same = (z // 4) == q
    both = jnp.where(same & ((z & 1) == 0), 1.0, 0.0)
    top = jnp.where(same & ((z & 3) == 3), 1.0, 0.0)
    m = 2
    ux = exact_dot(gxu[m + 1][rows], both)
    uy = exact_dot((gyu[m] + gyu[m + 1])[rows], both)
    uz = exact_dot((gzu[m] + gzu[m + 1])[rows], top)
    ue = exact_dot((medge[m] + medge[m + 1])[rows], both)
    own_cc[0] = cells(ux)
    own_cc[1] = jnp.concatenate([uy[2:3], uy[6:7]], axis=0)
    own_cc[2] = cells(uz)
    own_cc[3] = cells(ue)

    spot_cc = CC.at[:, i, pl.ds(2 * j, 2), :]
    spot_cb = CB.at[i, pl.ds(2 * j, 2), :]

    def spread(src, dst, which):
        def one(t, c):
            pltpu.make_async_remote_copy(
                src_ref=src, dst_ref=dst, send_sem=g_send.at[which], recv_sem=g_recv.at[which],
                device_id=other(t), device_id_type=MESH,
            ).start()
            return c

        lax.fori_loop(1, n, one, 0)
        pltpu.make_async_copy(src, dst, g_recv.at[which]).start()

    spread(own_cc, spot_cc, 0)

    each(2, "wait_recv")
    v1 = [V1[m] for m in range(nm)]
    v2 = [None] * nm
    for m in range(1, nm - 1):
        around = flow(gxu[m - 1], gxu[m], gyu[m], gzu[m], v1[m - 1], v1[m], v1[m + 1], 2)
        v2[m] = (1.0 + KEEP) * v1[m] + minv[m] * around
    for m in range(2, nm - 2):
        V2[m, rows, :] = v2[m][rows]
    total = None
    for m in range(2, nm - 2):
        around = flow(gxu[m - 1], gxu[m], gyu[m], gzu[m], v2[m - 1], v2[m], v2[m + 1], 2)
        r = mdiag[m] * (v1[m] * (1.0 / OMEGA) - v2[m]) + around
        total = r if total is None else total + r
    own_cb[...] = cells(exact_dot(total[rows], both))
    spread(own_cb, spot_cb, 1)
    each(3, "start")

    pltpu.make_async_copy(CC, CC, g_recv.at[0]).wait()
    cx, cy, cz, ce = CC[0], CC[1], CC[2], CC[3]

    def before(v):
        return jnp.concatenate([v[-1:], v[:-1]], axis=0)

    def after(v):
        return jnp.concatenate([v[1:], v[:1]], axis=0)

    cxl = before(cx)
    cdiag = (cx + cxl) + (cy + shift(cy, 1, 1)) + (cz + shift(cz, 1, 2)) + ce
    cinv = OMEGA / cdiag
    cyl, czl = shift(cy, 1, 1) * cinv, shift(cz, 1, 2) * cinv
    cx, cxl, cy, cz = cx * cinv, cxl * cinv, cy * cinv, cz * cinv
    pltpu.make_async_copy(CB, CB, g_recv.at[1]).wait()
    b = CB[...] * cinv
    v = b
    for step in range(SWEEPS - 1):
        around = cxl * before(v) + cx * after(v)
        around = around + cyl * shift(v, 1, 1) + cy * shift(v, -1, 1)
        around = around + czl * shift(v, 1, 2) + cz * shift(v, -1, 2)
        v = KEEP * v + b + around
    zero = jnp.zeros((1,) + v.shape[1:], jnp.float32)
    CR[0:1] = zero
    CR[gx + 1:gx + 2] = zero
    CR[1:gx + 1] = v

    crow = CR.shape[1]
    er = lax.broadcasted_iota(jnp.int32, (tile[0], crow), 0)
    ec = lax.broadcasted_iota(jnp.int32, (tile[0], crow), 1)
    pick = jnp.where(ec == 2 * j - 1 + er // 4, 1.0, 0.0)
    near = jnp.concatenate([exact_dot(pick, CR[i + p]) for p in range(3)], axis=0)
    zq = lax.broadcasted_iota(jnp.int32, (nz // 4, nz), 0)
    zz = lax.broadcasted_iota(jnp.int32, (nz // 4, nz), 1)
    near = exact_dot(near, jnp.where(zz // 4 == zq, 1.0, 0.0))
    near = near.reshape(3, *tile)
    each(3, "wait_recv")
    w = [V2[m] + near[m // 2] for m in range(nm)]
    v3 = [None] * nm
    for m in range(1, nm - 1):
        around = flow(gxu[m - 1], gxu[m], gyu[m], gzu[m], w[m - 1], w[m], w[m + 1], 2)
        v3[m] = KEEP * w[m] + v1[m] + minv[m] * around
    f = [None] * nk
    for x in range(2, nk - 2):
        f[x] = u2[x] + v3[(x + 1) // 2]
    for x in range(3, nk - 3):
        around = flow(hx[x - 1], hx[x], hy[x], hz[x], f[x - 1], f[x], f[x + 1], 1)
        out_ref[x - 3] = (KEEP * f[x] + u1[x] + inv[x] * around)[rows]

    for which in range(4):
        each(which, "wait_send")
    pltpu.make_async_copy(bytes_cc, bytes_cc, g_send.at[0]).wait()
    pltpu.make_async_copy(bytes_cb, bytes_cb, g_send.at[1]).wait()


def shards(gx, gy, right_side, labels, conduct_table):
    nx, ny, nz = right_side.shape
    n = gx * gy
    deep = 2 * ROW0 + ny
    cy, cz = gy * (ny // 4), nz // 4
    f32 = jnp.float32
    return pl.pallas_call(
        functools.partial(kernel, gx, gy, nx, ny),
        out_shape=jax.ShapeDtypeStruct(right_side.shape, f32),
        in_specs=[
            pl.BlockSpec(memory_space=pltpu.VMEM),
            pl.BlockSpec(memory_space=pltpu.VMEM),
            pl.BlockSpec(memory_space=pltpu.SMEM),
        ],
        out_specs=pl.BlockSpec(memory_space=pltpu.VMEM),
        scratch_shapes=[
            pltpu.VMEM((nx + 6, deep, nz), f32),
            pltpu.VMEM((nx + 4, deep, nz), f32),
            pltpu.VMEM((nx // 2 + 4, deep, nz), f32),
            pltpu.VMEM((nx // 2 + 4, deep, nz), f32),
            pltpu.VMEM((4, gx, cy, cz), f32),
            pltpu.VMEM((gx, cy, cz), f32),
            pltpu.VMEM((gx + 2, cy, cz), f32),
            pltpu.VMEM((4, 2, cz), f32),
            pltpu.VMEM((2, cz), f32),
            pltpu.VMEM((n - 1, 8, cz), f32),
            pltpu.VMEM((n - 1, 2, cz), f32),
            pltpu.SemaphoreType.DMA((4, 8)),
            pltpu.SemaphoreType.DMA((4, 8)),
            pltpu.SemaphoreType.DMA((2,)),
            pltpu.SemaphoreType.DMA((2,)),
        ],
        compiler_params=pltpu.CompilerParams(
            collective_id=0, has_side_effects=True, vmem_limit_bytes=48 * 1024 * 1024
        ),
    )(right_side, labels, conduct_table)


def solution(mesh):
    in_specs = (P("gx", "gy", None), P("gx", "gy", None), P())
    return jax.shard_map(
        functools.partial(shards, mesh.shape["gx"], mesh.shape["gy"]),
        mesh=mesh,
        in_specs=in_specs,
        out_specs=P("gx", "gy", None),
        check_vma=False,
    )
```

time: 284 us -> 25.3 us (0.09); the launches traced: 280 us -> 25.1 us
  starting transfers between devices: 112 us -> 0 us
  waiting for transfers between devices: 96.3 us -> 0 us
  local copies, waits for them, and re-layouts: 50.3 us -> 2.96 us
  Pallas kernels: 0 us -> 22.2 us
  other arithmetic: 20.4 us -> 0 us
    ppermute x56 -> x0, starting transfers between devices: 112 us -> none  [the longest x28 75.6 us: extended(): lax.ppermute(tail, axis, [(i, (i + 1) % count) for i in range(ends)])]
    ppermute x56 -> x0, waiting for transfers between devices: 96.3 us -> none  [the longest x28 96.1 us: extended(): lax.ppermute(head, axis, [((i + 1) % count, i) for i in range(ends)])]
    squeeze x12 -> x0, local copies, waits for them, and re-layouts: 36.2 us -> none  [the longest x2 6.09 us: coarsen_couplings(): lower_one = jnp.sum(blocks[0][:, 0], axis=(2, 4))]
    pallas_call x0 -> x1, Pallas kernels: none -> 22.2 us  [shards(): pl.pallas_call(functools.partial(kernel, gx, gy, nx, ny), out_shape=jax.S...]
    reduce_sum x12 -> x0, other arithmetic: 12.9 us -> none  [the longest x2 6.17 us: coarsen_couplings(): upper_three = jnp.sum(blocks[5][..., 1], axis=(1, 3))]
    reshape x2 -> x0, local copies, waits for them, and re-layouts: 9.58 us -> none  [the longest x1 5.55 us: restrict(): field.reshape(extent[0] // 2, 2, extent[1] // 2, 2, extent[2] // 2, 2)]
    unnamed x7, local copies, waits for them, and re-layouts: 0.02 us -> 2.96 us
  transfers between devices with their start and end apart: 56 -> 0, of which waited for: 29 -> 0; matrix products, arithmetic and copies ran while one was open for 9% -> 0% of each run, Pallas kernels for 0% -> 0%
where the time goes in v1:
time: 25.3 us; the launch traced here: 25.1 us
  Pallas kernels  22.2 us (88%)
  local copies, waits for them, and re-layouts  2.96 us (12%)
    pallas_call x1, Pallas kernels, shards(): pl.pallas_call(functools.partial(kernel, gx, gy, nx, ny), out_shape=jax.S...  22.2 us
    unnamed x7, local copies, waits for them, and re-layouts  2.96 us

profile of v1, /device:TPU:0, one launch (start us, length us, event | category | flops | bytes accessed | tf_op | source)
XLA Modules:
  0.0 25.1 jit_solution(12087391057014314564)
XLA Ops:
  0.0 0.0 copy-start
  0.0 0.8 %copy-done = f32[4,8,512]{2,1,0:T(8,128)S(1)} copy-done((f32[4,8,512]{2,1,0:T(8,128)S(1)}, f32[4,8,512]{2,1,0:T(8,128)}, u32[]{:S(2)}) %copy-start) | copy-done | bytes 65560
  0.8 0.0 copy-start.1
  0.8 0.8 %copy-done.1 = s32[4,8,512]{2,1,0:T(8,128)S(1)} copy-done((s32[4,8,512]{2,1,0:T(8,128)S(1)}, s32[4,8,512]{2,1,0:T(8,128)}, u32[]{:S(2)}) %copy-start.1) | copy-done | bytes 65560
  1.7 0.0 copy-start.2
  1.7 0.7 %copy-done.2 = f32[3]{0:T(128)S(1)} copy-done((f32[3]{0:T(128)S(1)}, f32[3]{0:T(128)}, u32[]{:S(2)}) %copy-start.2) | copy-done | bytes 36
  2.3 22.2 %shard_map.37 = f32[4,8,512]{2,1,0:T(8,128)S(1)} custom-call(f32[4,8,512]{2,1,0:T(8,128)S(1)} %copy-done, s32[4,8,512]{2,1,0:T(8,128)S(1)} %copy-done.1, f32[3]{0:T(128)S(1)} %copy-done.2), custom_call_target="tpu_custom_call" | custom-call | tf_op jit(solution)/shard_map/pallas_call | solution.py:296
  24.5 0.6 %copy.5 = f32[4,8,512]{2,1,0:T(8,128)} copy(f32[4,8,512]{2,1,0:T(8,128)S(1)} %shard_map.37) | data formatting | bytes 131072
Async XLA Ops:
  0.0 0.8 %copy-start = (f32[4,8,512]{2,1,0:T(8,128)S(1)}, f32[4,8,512]{2,1,0:T(8,128)}, u32[]{:S(2)}) copy-start(f32[4,8,512]{2,1,0:T(8,128)} %rhs_ref.1) | copy-start | bytes 196612
  0.8 0.8 %copy-start.1 = (s32[4,8,512]{2,1,0:T(8,128)S(1)}, s32[4,8,512]{2,1,0:T(8,128)}, u32[]{:S(2)}) copy-start(s32[4,8,512]{2,1,0:T(8,128)} %lab_ref.1) | copy-start | bytes 196612
  1.7 0.7 %copy-start.2 = (f32[3]{0:T(128)S(1)}, f32[3]{0:T(128)}, u32[]{:S(2)}) copy-start(f32[3]{0:T(128)} %tab_ref.1) | copy-start | bytes 40

commit v2 on v1

--- a/solution.py
+++ b/solution.py
@@ -37,39 +37,87 @@
     return total + hz * shift(v, -s, b) + shift(hz * v, s, b)
 
 
-def exact_dot(a, b):
-    return jnp.dot(a, b, preferred_element_type=jnp.float32, precision=lax.Precision.HIGHEST)
-
-
-def kernel(gx, gy, nx, ny, rhs_ref, lab_ref, tab_ref, out_ref, K, R, V1, V2, CC, CB, CR, own_cc, own_cb,
-           bytes_cc, bytes_cb, send, recv, g_send, g_recv):
+def turn(v, by, axis):
+    tile = 8 if axis == 0 else 128
+    parts = [lax.slice_in_dim(v, p, p + tile, axis=axis) for p in range(0, v.shape[axis], tile)]
+    return jnp.concatenate([pltpu.roll(p, by % tile, axis) for p in parts], axis=axis)
+
+
+def inverse(d):
+    r = pl.reciprocal(d, approx=True)
+    return r * (2.0 - d * r)
+
+
+def harmonic(a, b):
+    return (2.0 * (a * b)) * inverse(a + b)
+
+
+def exact_dot(a, ones):
+    rounded = lambda x: x.astype(jnp.bfloat16).astype(jnp.float32)
+    head = rounded(a)
+    rest = a - head
+    middle = rounded(rest)
+    parts = jnp.concatenate([head, middle, rest - middle], axis=0).astype(jnp.bfloat16)
+    out = jnp.dot(parts, ones, preferred_element_type=jnp.float32)
+    n = a.shape[0]
+    return out[:n] + out[n:2 * n] + out[2 * n:]
+
+
+def kernel(gx, gy, nx, ny, rhs_hbm, lab_hbm, tab_hbm, out_ref, K, R, V1, V2, CC, CB, CR, own_cc, own_cb,
+           bytes_cc, bytes_cb, lab_ref, tab_ref, to_cell, to_lane, send, recv, g_send, g_recv, fetch):
     i = lax.axis_index("gx")
     j = lax.axis_index("gy")
     n = gx * gy
     me = i * gy + j
-    nz = rhs_ref.shape[2]
+    nz = lab_ref.shape[2]
     mx = nx // 2
     tile = (2 * ROW0 + ny, nz)
-
-    for buf in (K, R, V1, V2):
+    rows = slice(ROW0, ROW0 + ny)
+
+    get_lab = pltpu.make_async_copy(lab_hbm, lab_ref, fetch.at[0])
+    get_tab = pltpu.make_async_copy(tab_hbm, tab_ref, fetch.at[1])
+    get_rhs = pltpu.make_async_copy(rhs_hbm, R.at[2:2 + nx, rows, :], fetch.at[2])
+    get_lab.start()
+    get_tab.start()
+
+    K[...] = jnp.full(K.shape, TINY, jnp.float32)
+    for buf in (R, V1, V2):
         buf[...] = jnp.zeros(buf.shape, jnp.float32)
 
-    def other(k):
-        t = lax.rem(me + k, n)
-        return (t // gy, lax.rem(t, gy))
+    def for_others(what):
+        if n <= 64:
+            ti = [i] + [lax.rem(i + a, gx) for a in range(1, gx)]
+            tj = [j] + [lax.rem(j + b, gy) for b in range(1, gy)]
+            for b in reversed(range(gy)):
+                for a in range(gx):
+                    if a or b:
+                        what((ti[a], tj[b]))
+        else:
+            def one(k, c):
+                t = lax.rem(me + k, n)
+                what((lax.div(t, gy), lax.rem(t, gy)))
+                return c
+
+            lax.fori_loop(1, n, one, 0)
 
     barrier = pltpu.get_barrier_semaphore()
-
-    def greet(k, c):
-        pl.semaphore_signal(barrier, inc=1, device_id=other(k), device_id_type=MESH)
-        return c
-
-    lax.fori_loop(1, n, greet, 0)
-    rows = slice(ROW0, ROW0 + ny)
+    for_others(lambda dev: pl.semaphore_signal(barrier, inc=1, device_id=dev, device_id_type=MESH))
+    get_rhs.start()
+
+    z = lax.broadcasted_iota(jnp.int32, (nz, nz // 4), 0)
+    q = lax.broadcasted_iota(jnp.int32, (nz, nz // 4), 1)
+    to_cell[...] = jnp.where(((z >> 2) == q) & ((z & 1) == 0), 1.0, 0.0).astype(jnp.bfloat16)
+    q = lax.broadcasted_iota(jnp.int32, (nz // 4, nz), 0)
+    z = lax.broadcasted_iota(jnp.int32, (nz // 4, nz), 1)
+    to_lane[...] = jnp.where((z >> 2) == q, 1.0, 0.0).astype(jnp.bfloat16)
+    CR[...] = jnp.zeros(CR.shape, jnp.float32)
+
+    get_lab.wait()
+    get_tab.wait()
     t0, t1, t2 = tab_ref[0], tab_ref[1], tab_ref[2]
     labels = lab_ref[...]
     K[3:3 + nx, rows, :] = jnp.where(labels == 0, t0, jnp.where(labels == 1, t1, t2))
-    R[2:2 + nx, rows, :] = rhs_ref[...]
+    get_rhs.wait()
     pl.semaphore_wait(barrier, n - 1)
 
     def there(dx, dy):
@@ -122,32 +170,30 @@
 
     def pair(v, axis):
         odd = odd_row if axis == 0 else odd_lane
-        return v + jnp.where(odd, shift(v, 1, axis), shift(v, -1, axis))
+        return v + jnp.where(odd, turn(v, 1, axis), turn(v, -1, axis))
 
     def upper(v, axis):
         odd = odd_row if axis == 0 else odd_lane
-        return jnp.where(odd, v, shift(v, -1, axis))
+        return jnp.where(odd, v, turn(v, -1, axis))
+
+    one = lambda c: jnp.where(c, 1.0, 0.0)
+    faces = one(first_lane) + one(last_lane)
+    faces = faces + one((row == ROW0) & (j == 0)) + one((row == ROW0 + ny - 1) & (j == gy - 1))
+    x_faces = {3: one(i == 0), 2 + nx: one(i == gx - 1)}
 
     each(0, "wait_recv")
     nk = nx + 6
     k = [K[x] for x in range(nk)]
-
-    def harmonic(a, b):
-        return 2.0 * (a * b) / jnp.maximum(a + b, TINY)
 
     hx = [harmonic(k[x], k[x + 1]) for x in range(nk - 1)]
     hy, hz, edge, diag, inv = ([None] * nk for _ in range(5))
     for x in range(1, nk - 1):
         a = k[x]
-        y_up, y_low = shift(a, -1, 0), shift(a, 1, 0)
-        z_up = jnp.where(last_lane, 0.0, shift(a, -1, 1))
-        hy[x] = harmonic(a, y_up)
-        hz[x] = harmonic(a, z_up)
-        beyond = jnp.where(k[x - 1] > 0.0, 0.0, a) + jnp.where(k[x + 1] > 0.0, 0.0, a)
-        beyond = beyond + jnp.where(y_up > 0.0, 0.0, a) + jnp.where(y_low > 0.0, 0.0, a)
-        edge[x] = beyond + jnp.where(first_lane, a, 0.0) + jnp.where(last_lane, a, 0.0)
+        hy[x] = harmonic(a, shift(a, -1, 0))
+        hz[x] = harmonic(a, jnp.where(last_lane, 0.0, shift(a, -1, 1)))
+        edge[x] = a * ((faces + x_faces[x]) if x in x_faces else faces)
         diag[x] = (hx[x - 1] + hx[x]) + (hy[x] + shift(hy[x], 1, 0)) + (hz[x] + shift(hz[x], 1, 1)) + edge[x]
-        inv[x] = OMEGA / jnp.maximum(diag[x], TINY)
+        inv[x] = OMEGA * inverse(jnp.maximum(diag[x], TINY))
 
     nm = mx + 4
     gxu = [None] * nm
@@ -161,7 +207,7 @@
         medge[m] = pair(pair(edge[x] + edge[x + 1], 0), 1)
         mdiag[m] = (gxu[m - 1] + gxu[m]) + (gyu[m] + shift(gyu[m], 2, 0))
         mdiag[m] = mdiag[m] + (gzu[m] + shift(gzu[m], 2, 1)) + medge[m]
-        minv[m] = OMEGA / jnp.maximum(mdiag[m], TINY)
+        minv[m] = OMEGA * inverse(jnp.maximum(mdiag[m], TINY))
 
     each(1, "wait_recv")
     u1, u2 = [None] * nk, [None] * nk
@@ -184,16 +230,11 @@
     def cells(v):
         return jnp.concatenate([v[0:1] + v[2:3], v[4:5] + v[6:7]], axis=0)
 
-    z = lax.broadcasted_iota(jnp.int32, (nz, nz // 4), 0)
-    q = lax.broadcasted_iota(jnp.int32, (nz, nz // 4), 1)
-    same = (z // 4) == q
-    both = jnp.where(same & ((z & 1) == 0), 1.0, 0.0)
-    top = jnp.where(same & ((z & 3) == 3), 1.0, 0.0)
     m = 2
-    ux = exact_dot(gxu[m + 1][rows], both)
-    uy = exact_dot((gyu[m] + gyu[m + 1])[rows], both)
-    uz = exact_dot((gzu[m] + gzu[m + 1])[rows], top)
-    ue = exact_dot((medge[m] + medge[m + 1])[rows], both)
+    uz = jnp.where((lane & 2) == 2, gzu[m] + gzu[m + 1], 0.0)
+    parts = (gxu[m + 1], gyu[m] + gyu[m + 1], uz, medge[m] + medge[m + 1])
+    got = exact_dot(jnp.concatenate([p[rows] for p in parts], axis=0), to_cell[...])
+    ux, uy, uz, ue = (got[p * ny:(p + 1) * ny] for p in range(4))
     own_cc[0] = cells(ux)
     own_cc[1] = jnp.concatenate([uy[2:3], uy[6:7]], axis=0)
     own_cc[2] = cells(uz)
@@ -203,14 +244,10 @@
     spot_cb = CB.at[i, pl.ds(2 * j, 2), :]
 
     def spread(src, dst, which):
-        def one(t, c):
-            pltpu.make_async_remote_copy(
-                src_ref=src, dst_ref=dst, send_sem=g_send.at[which], recv_sem=g_recv.at[which],
-                device_id=other(t), device_id_type=MESH,
-            ).start()
-            return c
-
-        lax.fori_loop(1, n, one, 0)
+        for_others(lambda dev: pltpu.make_async_remote_copy(
+            src_ref=src, dst_ref=dst, send_sem=g_send.at[which], recv_sem=g_recv.at[which],
+            device_id=dev, device_id_type=MESH,
+        ).start())
         pltpu.make_async_copy(src, dst, g_recv.at[which]).start()
 
     spread(own_cc, spot_cc, 0)
@@ -228,7 +265,7 @@
         around = flow(gxu[m - 1], gxu[m], gyu[m], gzu[m], v2[m - 1], v2[m], v2[m + 1], 2)
         r = mdiag[m] * (v1[m] * (1.0 / OMEGA) - v2[m]) + around
         total = r if total is None else total + r
-    own_cb[...] = cells(exact_dot(total[rows], both))
+    own_cb[...] = cells(exact_dot(total[rows], to_cell[...]))
     spread(own_cb, spot_cb, 1)
     each(3, "start")
 
@@ -243,7 +280,7 @@
 
     cxl = before(cx)
     cdiag = (cx + cxl) + (cy + shift(cy, 1, 1)) + (cz + shift(cz, 1, 2)) + ce
-    cinv = OMEGA / cdiag
+    cinv = OMEGA * inverse(cdiag)
     cyl, czl = shift(cy, 1, 1) * cinv, shift(cz, 1, 2) * cinv
     cx, cxl, cy, cz = cx * cinv, cxl * cinv, cy * cinv, cz * cinv
     pltpu.make_async_copy(CB, CB, g_recv.at[1]).wait()
@@ -254,20 +291,14 @@
         around = around + cyl * shift(v, 1, 1) + cy * shift(v, -1, 1)
         around = around + czl * shift(v, 1, 2) + cz * shift(v, -1, 2)
         v = KEEP * v + b + around
-    zero = jnp.zeros((1,) + v.shape[1:], jnp.float32)
-    CR[0:1] = zero
-    CR[gx + 1:gx + 2] = zero
-    CR[1:gx + 1] = v
-
-    crow = CR.shape[1]
-    er = lax.broadcasted_iota(jnp.int32, (tile[0], crow), 0)
-    ec = lax.broadcasted_iota(jnp.int32, (tile[0], crow), 1)
-    pick = jnp.where(ec == 2 * j - 1 + er // 4, 1.0, 0.0)
-    near = jnp.concatenate([exact_dot(pick, CR[i + p]) for p in range(3)], axis=0)
-    zq = lax.broadcasted_iota(jnp.int32, (nz // 4, nz), 0)
-    zz = lax.broadcasted_iota(jnp.int32, (nz // 4, nz), 1)
-    near = exact_dot(near, jnp.where(zz // 4 == zq, 1.0, 0.0))
-    near = near.reshape(3, *tile)
+    CR[1:gx + 1, 8:8 + v.shape[1], :] = v
+
+    near = [CR[i + p, pl.ds(7 + 2 * j + c, 1), :] for p in range(3) for c in range(4)]
+    near = exact_dot(jnp.concatenate(near + [jnp.zeros((4, nz // 4), jnp.float32)], axis=0), to_lane[...])
+    near = [
+        jnp.concatenate([jnp.broadcast_to(near[4 * p + c:4 * p + c + 1], (4, nz)) for c in range(4)], axis=0)
+        for p in range(3)
+    ]
     each(3, "wait_recv")
     w = [V2[m] + near[m // 2] for m in range(nm)]
     v3 = [None] * nm
@@ -297,9 +328,9 @@
         functools.partial(kernel, gx, gy, nx, ny),
         out_shape=jax.ShapeDtypeStruct(right_side.shape, f32),
         in_specs=[
-            pl.BlockSpec(memory_space=pltpu.VMEM),
-            pl.BlockSpec(memory_space=pltpu.VMEM),
-            pl.BlockSpec(memory_space=pltpu.SMEM),
+            pl.BlockSpec(memory_space=pltpu.HBM),
+            pl.BlockSpec(memory_space=pltpu.HBM),
+            pl.BlockSpec(memory_space=pltpu.HBM),
         ],
         out_specs=pl.BlockSpec(memory_space=pltpu.VMEM),
         scratch_shapes=[
@@ -309,18 +340,23 @@
             pltpu.VMEM((nx // 2 + 4, deep, nz), f32),
             pltpu.VMEM((4, gx, cy, cz), f32),
             pltpu.VMEM((gx, cy, cz), f32),
-            pltpu.VMEM((gx + 2, cy, cz), f32),
+            pltpu.VMEM((gx + 2, cy + 16, cz), f32),
             pltpu.VMEM((4, 2, cz), f32),
             pltpu.VMEM((2, cz), f32),
             pltpu.VMEM((n - 1, 8, cz), f32),
             pltpu.VMEM((n - 1, 2, cz), f32),
+            pltpu.VMEM((nx, ny, nz), jnp.int32),
+            pltpu.SMEM((3,), f32),
+            pltpu.VMEM((nz, cz), jnp.bfloat16),
+            pltpu.VMEM((cz, nz), jnp.bfloat16),
             pltpu.SemaphoreType.DMA((4, 8)),
             pltpu.SemaphoreType.DMA((4, 8)),
             pltpu.SemaphoreType.DMA((2,)),
             pltpu.SemaphoreType.DMA((2,)),
+            pltpu.SemaphoreType.DMA((3,)),
         ],
         compiler_params=pltpu.CompilerParams(
-            collective_id=0, has_side_effects=True, vmem_limit_bytes=48 * 1024 * 1024
+            collective_id=0, has_side_effects=True, vmem_limit_bytes=64 * 1024 * 1024
         ),
     )(right_side, labels, conduct_table)
 

time: 25.3 us -> 23.1 us (0.913)
  local copies, waits for them, and re-layouts: 2.96 us -> 1.47 us
  Pallas kernels: 22.2 us -> 21.4 us
    unnamed x7 -> x1, local copies, waits for them, and re-layouts: 2.96 us -> 1.47 us
    pallas_call x1, Pallas kernels: 22.2 us -> 21.4 us  [shards(): pl.pallas_call(functools.partial(kernel, gx, gy, nx, ny), out_shape=jax.S...]
where the time goes in v2:
time: 23.1 us; the launch traced here: 22.9 us
  Pallas kernels  21.4 us (93%)
  local copies, waits for them, and re-layouts  1.47 us (6%)
    pallas_call x1, Pallas kernels, shards(): pl.pallas_call(functools.partial(kernel, gx, gy, nx, ny), out_shape=jax.S...  21.4 us
    unnamed x1, local copies, waits for them, and re-layouts  1.47 us

profile of v2, /device:TPU:0, one launch (start us, length us, event | category | flops | bytes accessed | tf_op | source)
XLA Modules:
  0.0 22.9 jit_solution(11267672536576899833)
XLA Ops:
  0.0 21.4 %shard_map.37 = f32[4,8,512]{2,1,0:T(8,128)} custom-call(f32[4,8,512]{2,1,0:T(8,128)} %rhs_hbm.1, s32[4,8,512]{2,1,0:T(8,128)} %lab_hbm.1, f32[3]{0:T(128)} %tab_hbm.1), custom_call_target="tpu_custom_call" | custom-call | tf_op jit(solution)/shard_map/pallas_call | solution.py:327
  21.4 1.5 %copy.5 = f32[4,8,512]{2,1,0:T(8,128)} copy(f32[4,8,512]{2,1,0:T(8,128)} %shard_map.37) | data formatting | bytes 131072

commit v3 on v2

--- a/solution.py
+++ b/solution.py
@@ -64,7 +64,7 @@
 
 
 def kernel(gx, gy, nx, ny, rhs_hbm, lab_hbm, tab_hbm, out_ref, K, R, V1, V2, CC, CB, CR, own_cc, own_cb,
-           bytes_cc, bytes_cb, lab_ref, tab_ref, to_cell, to_lane, send, recv, g_send, g_recv, fetch):
+           bytes_cy, bytes_cx, bytes_cb, lab_ref, tab_ref, to_cell, to_lane, send, recv, g_send, g_recv, fetch):
     i = lax.axis_index("gx")
     j = lax.axis_index("gy")
     n = gx * gy
@@ -209,6 +209,34 @@
         mdiag[m] = mdiag[m] + (gzu[m] + shift(gzu[m], 2, 1)) + medge[m]
         minv[m] = OMEGA * inverse(jnp.maximum(mdiag[m], TINY))
 
+    def cells(v):
+        return jnp.concatenate([v[0:1] + v[2:3], v[4:5] + v[6:7]], axis=0)
+
+    m = 2
+    uz = jnp.where((lane & 2) == 2, gzu[m] + gzu[m + 1], 0.0)
+    parts = (gxu[m + 1], gyu[m] + gyu[m + 1], uz, medge[m] + medge[m + 1])
+    got = exact_dot(jnp.concatenate([p[rows] for p in parts], axis=0), to_cell[...])
+    ux, uy, uz, ue = (got[p * ny:(p + 1) * ny] for p in range(4))
+    own_cc[0] = cells(ux)
+    own_cc[1] = jnp.concatenate([uy[2:3], uy[6:7]], axis=0)
+    own_cc[2] = cells(uz)
+    own_cc[3] = cells(ue)
+
+    along_gy = [(i, lax.rem(j + b, gy)) for b in range(1, gy)]
+    along_gx = [(lax.rem(i + a, gx), j) for a in range(1, gx)]
+    spot_cc = CC.at[:, i, pl.ds(2 * j, 2), :]
+    line_cc = CC.at[:, i]
+
+    def to_each(devices, src, dst, which):
+        for dev in devices:
+            pltpu.make_async_remote_copy(
+                src_ref=src, dst_ref=dst, send_sem=g_send.at[which], recv_sem=g_recv.at[which],
+                device_id=dev, device_id_type=MESH,
+            ).start()
+
+    to_each(along_gy, own_cc, spot_cc, 0)
+    pltpu.make_async_copy(own_cc, spot_cc, g_recv.at[0]).start()
+
     each(1, "wait_recv")
     u1, u2 = [None] * nk, [None] * nk
     for x in range(1, nk - 1):
@@ -227,30 +255,10 @@
         V1[m, rows, :] = (source * minv[m])[rows]
     each(2, "start")
 
-    def cells(v):
-        return jnp.concatenate([v[0:1] + v[2:3], v[4:5] + v[6:7]], axis=0)
-
-    m = 2
-    uz = jnp.where((lane & 2) == 2, gzu[m] + gzu[m + 1], 0.0)
-    parts = (gxu[m + 1], gyu[m] + gyu[m + 1], uz, medge[m] + medge[m + 1])
-    got = exact_dot(jnp.concatenate([p[rows] for p in parts], axis=0), to_cell[...])
-    ux, uy, uz, ue = (got[p * ny:(p + 1) * ny] for p in range(4))
-    own_cc[0] = cells(ux)
-    own_cc[1] = jnp.concatenate([uy[2:3], uy[6:7]], axis=0)
-    own_cc[2] = cells(uz)
-    own_cc[3] = cells(ue)
-
-    spot_cc = CC.at[:, i, pl.ds(2 * j, 2), :]
     spot_cb = CB.at[i, pl.ds(2 * j, 2), :]
 
-    def spread(src, dst, which):
-        for_others(lambda dev: pltpu.make_async_remote_copy(
-            src_ref=src, dst_ref=dst, send_sem=g_send.at[which], recv_sem=g_recv.at[which],
-            device_id=dev, device_id_type=MESH,
-        ).start())
-        pltpu.make_async_copy(src, dst, g_recv.at[which]).start()
-
-    spread(own_cc, spot_cc, 0)
+    pltpu.make_async_copy(line_cc, line_cc, g_recv.at[0]).wait()
+    to_each(along_gx, line_cc, line_cc, 1)
 
     each(2, "wait_recv")
     v1 = [V1[m] for m in range(nm)]
@@ -266,10 +274,14 @@
         r = mdiag[m] * (v1[m] * (1.0 / OMEGA) - v2[m]) + around
         total = r if total is None else total + r
     own_cb[...] = cells(exact_dot(total[rows], to_cell[...]))
-    spread(own_cb, spot_cb, 1)
+    for_others(lambda dev: pltpu.make_async_remote_copy(
+        src_ref=own_cb, dst_ref=spot_cb, send_sem=g_send.at[2], recv_sem=g_recv.at[2],
+        device_id=dev, device_id_type=MESH,
+    ).start())
+    pltpu.make_async_copy(own_cb, spot_cb, g_recv.at[2]).start()
     each(3, "start")
 
-    pltpu.make_async_copy(CC, CC, g_recv.at[0]).wait()
+    pltpu.make_async_copy(bytes_cx, bytes_cx, g_recv.at[1]).wait()
     cx, cy, cz, ce = CC[0], CC[1], CC[2], CC[3]
 
     def before(v):
@@ -283,7 +295,7 @@
     cinv = OMEGA * inverse(cdiag)
     cyl, czl = shift(cy, 1, 1) * cinv, shift(cz, 1, 2) * cinv
     cx, cxl, cy, cz = cx * cinv, cxl * cinv, cy * cinv, cz * cinv
-    pltpu.make_async_copy(CB, CB, g_recv.at[1]).wait()
+    pltpu.make_async_copy(CB, CB, g_recv.at[2]).wait()
     b = CB[...] * cinv
     v = b
     for step in range(SWEEPS - 1):
@@ -314,8 +326,8 @@
 
     for which in range(4):
         each(which, "wait_send")
-    pltpu.make_async_copy(bytes_cc, bytes_cc, g_send.at[0]).wait()
-    pltpu.make_async_copy(bytes_cb, bytes_cb, g_send.at[1]).wait()
+    for which, amount in enumerate((bytes_cy, bytes_cx, bytes_cb)):
+        pltpu.make_async_copy(amount, amount, g_send.at[which]).wait()
 
 
 def shards(gx, gy, right_side, labels, conduct_table):
@@ -343,7 +355,8 @@
             pltpu.VMEM((gx + 2, cy + 16, cz), f32),
             pltpu.VMEM((4, 2, cz), f32),
             pltpu.VMEM((2, cz), f32),
-            pltpu.VMEM((n - 1, 8, cz), f32),
+            pltpu.VMEM((gy - 1, 4, 2, cz), f32),
+            pltpu.VMEM((gx - 1, 4, cy, cz), f32),
             pltpu.VMEM((n - 1, 2, cz), f32),
             pltpu.VMEM((nx, ny, nz), jnp.int32),
             pltpu.SMEM((3,), f32),
@@ -351,14 +364,14 @@
             pltpu.VMEM((cz, nz), jnp.bfloat16),
             pltpu.SemaphoreType.DMA((4, 8)),
             pltpu.SemaphoreType.DMA((4, 8)),
-            pltpu.SemaphoreType.DMA((2,)),
-            pltpu.SemaphoreType.DMA((2,)),
+            pltpu.SemaphoreType.DMA((3,)),
+            pltpu.SemaphoreType.DMA((3,)),
             pltpu.SemaphoreType.DMA((3,)),
         ],
         compiler_params=pltpu.CompilerParams(
-            collective_id=0, has_side_effects=True, vmem_limit_bytes=64 * 1024 * 1024
+            collective_id=0, has_side_effects=True, vmem_limit_bytes=48 * 1024 * 1024
         ),
-    )(right_side, labels, conduct_table)
+    )(*(pltpu.with_memory_space_constraint(x, pltpu.HBM) for x in (right_side, labels, conduct_table)))
 
 
 def solution(mesh):

time: 23.1 us -> 21.7 us (0.939)
  local copies, waits for them, and re-layouts: 1.47 us -> 0.63 us
  Pallas kernels: 21.4 us -> 20.8 us
    unnamed x1, local copies, waits for them, and re-layouts: 1.47 us -> 0.63 us
    pallas_call x1, Pallas kernels: 21.4 us -> 20.8 us  [shards(): pl.pallas_call(functools.partial(kernel, gx, gy, nx, ny), out_shape=jax.S...]
where the time goes in v3:
time: 21.7 us; the launch traced here: 21.5 us
  Pallas kernels  20.8 us (96%)
  local copies, waits for them, and re-layouts  0.63 us (3%)
    pallas_call x1, Pallas kernels, shards(): pl.pallas_call(functools.partial(kernel, gx, gy, nx, ny), out_shape=jax.S...  20.8 us
    unnamed x1, local copies, waits for them, and re-layouts  0.63 us

profile of v3, /device:TPU:0, one launch (start us, length us, event | category | flops | bytes accessed | tf_op | source)
XLA Modules:
  0.0 21.5 jit_solution(10534748348349140128)
XLA Ops:
  0.0 20.8 %shard_map.37 = f32[4,8,512]{2,1,0:T(8,128)S(1)} custom-call(f32[4,8,512]{2,1,0:T(8,128)} %rhs_hbm.1, s32[4,8,512]{2,1,0:T(8,128)} %lab_hbm.1, f32[3]{0:T(128)} %tab_hbm.1), custom_call_target="tpu_custom_call" | custom-call | tf_op jit(solution)/shard_map/pallas_call | solution.py:339
  20.9 0.6 %copy.5 = f32[4,8,512]{2,1,0:T(8,128)} copy(f32[4,8,512]{2,1,0:T(8,128)S(1)} %shard_map.37) | data formatting | bytes 131072

commit v4 on v3

--- a/solution.py
+++ b/solution.py
@@ -198,10 +198,12 @@
     nm = mx + 4
     gxu = [None] * nm
     gyu, gzu, medge, mdiag, minv = ([None] * nm for _ in range(5))
-    for m in range(nm - 1):
-        gxu[m] = pair(pair(hx[2 * m], 0), 1)
-    for m in range(1, nm - 1):
+
+    def middle(m):
         x = 2 * m - 1
+        for t in (m - 1, m):
+            if gxu[t] is None:
+                gxu[t] = pair(pair(hx[2 * t], 0), 1)
         gyu[m] = upper(pair(hy[x] + hy[x + 1], 1), 0)
         gzu[m] = upper(pair(hz[x] + hz[x + 1], 0), 1)
         medge[m] = pair(pair(edge[x] + edge[x + 1], 0), 1)
@@ -209,33 +211,8 @@
         mdiag[m] = mdiag[m] + (gzu[m] + shift(gzu[m], 2, 1)) + medge[m]
         minv[m] = OMEGA * inverse(jnp.maximum(mdiag[m], TINY))
 
-    def cells(v):
-        return jnp.concatenate([v[0:1] + v[2:3], v[4:5] + v[6:7]], axis=0)
-
-    m = 2
-    uz = jnp.where((lane & 2) == 2, gzu[m] + gzu[m + 1], 0.0)
-    parts = (gxu[m + 1], gyu[m] + gyu[m + 1], uz, medge[m] + medge[m + 1])
-    got = exact_dot(jnp.concatenate([p[rows] for p in parts], axis=0), to_cell[...])
-    ux, uy, uz, ue = (got[p * ny:(p + 1) * ny] for p in range(4))
-    own_cc[0] = cells(ux)
-    own_cc[1] = jnp.concatenate([uy[2:3], uy[6:7]], axis=0)
-    own_cc[2] = cells(uz)
-    own_cc[3] = cells(ue)
-
-    along_gy = [(i, lax.rem(j + b, gy)) for b in range(1, gy)]
-    along_gx = [(lax.rem(i + a, gx), j) for a in range(1, gx)]
-    spot_cc = CC.at[:, i, pl.ds(2 * j, 2), :]
-    line_cc = CC.at[:, i]
-
-    def to_each(devices, src, dst, which):
-        for dev in devices:
-            pltpu.make_async_remote_copy(
-                src_ref=src, dst_ref=dst, send_sem=g_send.at[which], recv_sem=g_recv.at[which],
-                device_id=dev, device_id_type=MESH,
-            ).start()
-
-    to_each(along_gy, own_cc, spot_cc, 0)
-    pltpu.make_async_copy(own_cc, spot_cc, g_recv.at[0]).start()
+    for m in range(2, nm - 2):
+        middle(m)
 
     each(1, "wait_recv")
     u1, u2 = [None] * nk, [None] * nk
@@ -254,11 +231,38 @@
         source = pair(pair(res[x] + res[x + 1], 0), 1)
         V1[m, rows, :] = (source * minv[m])[rows]
     each(2, "start")
+    for m in (1, nm - 2):
+        middle(m)
+
+    def cells(v):
+        return jnp.concatenate([v[0:1] + v[2:3], v[4:5] + v[6:7]], axis=0)
+
+    m = 2
+    uz = jnp.where((lane & 2) == 2, gzu[m] + gzu[m + 1], 0.0)
+    parts = (gxu[m + 1], gyu[m] + gyu[m + 1], uz, medge[m] + medge[m + 1])
+    got = exact_dot(jnp.concatenate([p[rows] for p in parts], axis=0), to_cell[...])
+    ux, uy, uz, ue = (got[p * ny:(p + 1) * ny] for p in range(4))
+    own_cc[0] = cells(ux)
+    own_cc[1] = jnp.concatenate([uy[2:3], uy[6:7]], axis=0)
+    own_cc[2] = cells(uz)
+    own_cc[3] = cells(ue)
+
+    along_gy = [(i, lax.rem(j + b, gy)) for b in range(1, gy)]
+    along_gx = [(lax.rem(i + a, gx), j) for a in range(1, gx)]
+    spot_cc = CC.at[:, i, pl.ds(2 * j, 2), :]
+    line_cc = CC.at[:, i]
+
+    def to_each(devices, src, dst, which):
+        for dev in devices:
+            pltpu.make_async_remote_copy(
+                src_ref=src, dst_ref=dst, send_sem=g_send.at[which], recv_sem=g_recv.at[which],
+                device_id=dev, device_id_type=MESH,
+            ).start()
+
+    to_each(along_gy, own_cc, spot_cc, 0)
+    pltpu.make_async_copy(own_cc, spot_cc, g_recv.at[0]).start()
 
     spot_cb = CB.at[i, pl.ds(2 * j, 2), :]
-
-    pltpu.make_async_copy(line_cc, line_cc, g_recv.at[0]).wait()
-    to_each(along_gx, line_cc, line_cc, 1)
 
     each(2, "wait_recv")
     v1 = [V1[m] for m in range(nm)]
@@ -268,6 +272,8 @@
         v2[m] = (1.0 + KEEP) * v1[m] + minv[m] * around
     for m in range(2, nm - 2):
         V2[m, rows, :] = v2[m][rows]
+    pltpu.make_async_copy(line_cc, line_cc, g_recv.at[0]).wait()
+    to_each(along_gx, line_cc, line_cc, 1)
     total = None
     for m in range(2, nm - 2):
         around = flow(gxu[m - 1], gxu[m], gyu[m], gzu[m], v2[m - 1], v2[m], v2[m + 1], 2)

time: 21.7 us -> 21.9 us (level)
  no operation moved by 1% of the time
where the time goes in v4:
time: 21.9 us; the launch traced here: 21.7 us
  Pallas kernels  21 us (96%)
  local copies, waits for them, and re-layouts  0.63 us (3%)
    pallas_call x1, Pallas kernels, shards(): pl.pallas_call(functools.partial(kernel, gx, gy, nx, ny), out_shape=jax.S...  21 us
    unnamed x1, local copies, waits for them, and re-layouts  0.63 us

profile of v4, /device:TPU:0, one launch (start us, length us, event | category | flops | bytes accessed | tf_op | source)
XLA Modules:
  0.0 21.7 jit_solution(380584661984571683)
XLA Ops:
  0.0 21.0 %shard_map.37 = f32[4,8,512]{2,1,0:T(8,128)S(1)} custom-call(f32[4,8,512]{2,1,0:T(8,128)} %rhs_hbm.1, s32[4,8,512]{2,1,0:T(8,128)} %lab_hbm.1, f32[3]{0:T(128)} %tab_hbm.1), custom_call_target="tpu_custom_call" | custom-call | tf_op jit(solution)/shard_map/pallas_call | solution.py:345
  21.1 0.6 %copy.5 = f32[4,8,512]{2,1,0:T(8,128)} copy(f32[4,8,512]{2,1,0:T(8,128)S(1)} %shard_map.37) | data formatting | bytes 131072

commit v5 on v4

--- a/solution.py
+++ b/solution.py
@@ -301,6 +301,10 @@
     cinv = OMEGA * inverse(cdiag)
     cyl, czl = shift(cy, 1, 1) * cinv, shift(cz, 1, 2) * cinv
     cx, cxl, cy, cz = cx * cinv, cxl * cinv, cy * cinv, cz * cinv
+    for which in range(3):
+        each(which, "wait_send")
+    each(3, "wait_recv")
+    each(3, "wait_send")
     pltpu.make_async_copy(CB, CB, g_recv.at[2]).wait()
     b = CB[...] * cinv
     v = b
@@ -317,7 +321,6 @@
         jnp.concatenate([jnp.broadcast_to(near[4 * p + c:4 * p + c + 1], (4, nz)) for c in range(4)], axis=0)
         for p in range(3)
     ]
-    each(3, "wait_recv")
     w = [V2[m] + near[m // 2] for m in range(nm)]
     v3 = [None] * nm
     for m in range(1, nm - 1):
@@ -330,8 +333,6 @@
         around = flow(hx[x - 1], hx[x], hy[x], hz[x], f[x - 1], f[x], f[x + 1], 1)
         out_ref[x - 3] = (KEEP * f[x] + u1[x] + inv[x] * around)[rows]
 
-    for which in range(4):
-        each(which, "wait_send")
     for which, amount in enumerate((bytes_cy, bytes_cx, bytes_cb)):
         pltpu.make_async_copy(amount, amount, g_send.at[which]).wait()
 

time: 21.9 us -> 21.8 us (level)
  no operation moved by 1% of the time
where the time goes in v5:
time: 21.8 us; the launch traced here: 21.7 us
  Pallas kernels  21 us (96%)
  local copies, waits for them, and re-layouts  0.63 us (3%)
    pallas_call x1, Pallas kernels, shards(): pl.pallas_call(functools.partial(kernel, gx, gy, nx, ny), out_shape=jax.S...  21 us
    unnamed x1, local copies, waits for them, and re-layouts  0.63 us

profile of v5, /device:TPU:0, one launch (start us, length us, event | category | flops | bytes accessed | tf_op | source)
XLA Modules:
  0.0 21.7 jit_solution(15505090271636477687)
XLA Ops:
  0.0 21.0 %shard_map.37 = f32[4,8,512]{2,1,0:T(8,128)S(1)} custom-call(f32[4,8,512]{2,1,0:T(8,128)} %rhs_hbm.1, s32[4,8,512]{2,1,0:T(8,128)} %lab_hbm.1, f32[3]{0:T(128)} %tab_hbm.1), custom_call_target="tpu_custom_call" | custom-call | tf_op jit(solution)/shard_map/pallas_call | solution.py:346
  21.0 0.6 %copy.5 = f32[4,8,512]{2,1,0:T(8,128)} copy(f32[4,8,512]{2,1,0:T(8,128)S(1)} %shard_map.37) | data formatting | bytes 131072

commit v6 on v5

--- a/solution.py
+++ b/solution.py
@@ -64,7 +64,8 @@
 
 
 def kernel(gx, gy, nx, ny, rhs_hbm, lab_hbm, tab_hbm, out_ref, K, R, V1, V2, CC, CB, CR, own_cc, own_cb,
-           bytes_cy, bytes_cx, bytes_cb, lab_ref, tab_ref, to_cell, to_lane, send, recv, g_send, g_recv, fetch):
+           bytes_cy, bytes_cx, bytes_cb, lab_ref, tab_ref, to_cell, to_lane, send, recv, g_send, g_recv, fetch,
+           HX, HY, HZ, EDGE, DIAG, INV, U1, U2, U3, GX, GY, GZ, MEDGE, MDIAG, MINV, T):
     i = lax.axis_index("gx")
     j = lax.axis_index("gy")
     n = gx * gy
@@ -179,67 +180,77 @@
     one = lambda c: jnp.where(c, 1.0, 0.0)
     faces = one(first_lane) + one(last_lane)
     faces = faces + one((row == ROW0) & (j == 0)) + one((row == ROW0 + ny - 1) & (j == gy - 1))
-    x_faces = {3: one(i == 0), 2 + nx: one(i == gx - 1)}
+    x_low, x_high = one(i == 0), one(i == gx - 1)
+
+    def over(first, last, body):
+        def step(x, c):
+            body(x)
+            return c
+
+        lax.fori_loop(first, last, step, 0)
 
     each(0, "wait_recv")
     nk = nx + 6
-    k = [K[x] for x in range(nk)]
-
-    hx = [harmonic(k[x], k[x + 1]) for x in range(nk - 1)]
-    hy, hz, edge, diag, inv = ([None] * nk for _ in range(5))
-    for x in range(1, nk - 1):
-        a = k[x]
-        hy[x] = harmonic(a, shift(a, -1, 0))
-        hz[x] = harmonic(a, jnp.where(last_lane, 0.0, shift(a, -1, 1)))
-        edge[x] = a * ((faces + x_faces[x]) if x in x_faces else faces)
-        diag[x] = (hx[x - 1] + hx[x]) + (hy[x] + shift(hy[x], 1, 0)) + (hz[x] + shift(hz[x], 1, 1)) + edge[x]
-        inv[x] = OMEGA * inverse(jnp.maximum(diag[x], TINY))
+    HX[0] = harmonic(K[0], K[1])
+
+    def fine(x):
+        a = K[x]
+        high = harmonic(a, K[x + 1])
+        hy = harmonic(a, shift(a, -1, 0))
+        hz = harmonic(a, jnp.where(last_lane, 0.0, shift(a, -1, 1)))
+        edge = a * (faces + (jnp.where(x == 3, x_low, 0.0) + jnp.where(x == 2 + nx, x_high, 0.0)))
+        diag = (HX[x - 1] + high) + (hy + shift(hy, 1, 0)) + (hz + shift(hz, 1, 1)) + edge
+        HX[x], HY[x], HZ[x], EDGE[x], DIAG[x] = high, hy, hz, edge, diag
+        INV[x] = OMEGA * inverse(jnp.maximum(diag, TINY))
+
+    over(1, nk - 1, fine)
 
     nm = mx + 4
-    gxu = [None] * nm
-    gyu, gzu, medge, mdiag, minv = ([None] * nm for _ in range(5))
+    GX[0] = pair(pair(HX[0], 0), 1)
 
     def middle(m):
         x = 2 * m - 1
-        for t in (m - 1, m):
-            if gxu[t] is None:
-                gxu[t] = pair(pair(hx[2 * t], 0), 1)
-        gyu[m] = upper(pair(hy[x] + hy[x + 1], 1), 0)
-        gzu[m] = upper(pair(hz[x] + hz[x + 1], 0), 1)
-        medge[m] = pair(pair(edge[x] + edge[x + 1], 0), 1)
-        mdiag[m] = (gxu[m - 1] + gxu[m]) + (gyu[m] + shift(gyu[m], 2, 0))
-        mdiag[m] = mdiag[m] + (gzu[m] + shift(gzu[m], 2, 1)) + medge[m]
-        minv[m] = OMEGA * inverse(jnp.maximum(mdiag[m], TINY))
-
-    for m in range(2, nm - 2):
-        middle(m)
+        gx_high = pair(pair(HX[x + 1], 0), 1)
+        gyu = upper(pair(HY[x] + HY[x + 1], 1), 0)
+        gzu = upper(pair(HZ[x] + HZ[x + 1], 0), 1)
+        edge = pair(pair(EDGE[x] + EDGE[x + 1], 0), 1)
+        diag = (GX[m - 1] + gx_high) + (gyu + shift(gyu, 2, 0)) + (gzu + shift(gzu, 2, 1)) + edge
+        GX[m], GY[m], GZ[m], MEDGE[m], MDIAG[m] = gx_high, gyu, gzu, edge, diag
+        MINV[m] = OMEGA * inverse(jnp.maximum(diag, TINY))
+
+    over(1, nm - 1, middle)
 
     each(1, "wait_recv")
-    u1, u2 = [None] * nk, [None] * nk
-    for x in range(1, nk - 1):
-        u1[x] = R[x - 1] * inv[x]
-    for x in range(2, nk - 2):
-        around = flow(hx[x - 1], hx[x], hy[x], hz[x], u1[x - 1], u1[x], u1[x + 1], 1)
-        u2[x] = (1.0 + KEEP) * u1[x] + inv[x] * around
-    res = [None] * nk
-    for x in range(3, nk - 3):
-        around = flow(hx[x - 1], hx[x], hy[x], hz[x], u2[x - 1], u2[x], u2[x + 1], 1)
-        res[x] = diag[x] * (u1[x] * (1.0 / OMEGA) - u2[x]) + around
-
-    for m in range(2, nm - 2):
+
+    def source(x):
+        U1[x] = R[x - 1] * INV[x]
+
+    def fine_flow(x, v):
+        return flow(HX[x - 1], HX[x], HY[x], HZ[x], v[x - 1], v[x], v[x + 1], 1)
+
+    def middle_flow(m, v):
+        return flow(GX[m - 1], GX[m], GY[m], GZ[m], v[m - 1], v[m], v[m + 1], 2)
+
+    def second(x):
+        U2[x] = (1.0 + KEEP) * U1[x] + INV[x] * fine_flow(x, U1)
+
+    def residual(x):
+        return DIAG[x] * (U1[x] * (1.0 / OMEGA) - U2[x]) + fine_flow(x, U2)
+
+    def restricted(m):
         x = 2 * m - 1
-        source = pair(pair(res[x] + res[x + 1], 0), 1)
-        V1[m, rows, :] = (source * minv[m])[rows]
+        V1[m, rows, :] = (pair(pair(residual(x) + residual(x + 1), 0), 1) * MINV[m])[rows]
+
+    over(1, nk - 1, source)
+    over(2, nk - 2, second)
+    over(2, nm - 2, restricted)
     each(2, "start")
-    for m in (1, nm - 2):
-        middle(m)
-
     def cells(v):
         return jnp.concatenate([v[0:1] + v[2:3], v[4:5] + v[6:7]], axis=0)
 
     m = 2
-    uz = jnp.where((lane & 2) == 2, gzu[m] + gzu[m + 1], 0.0)
-    parts = (gxu[m + 1], gyu[m] + gyu[m + 1], uz, medge[m] + medge[m + 1])
+    uz = jnp.where((lane & 2) == 2, GZ[m] + GZ[m + 1], 0.0)
+    parts = (GX[m + 1], GY[m] + GY[m + 1], uz, MEDGE[m] + MEDGE[m + 1])
     got = exact_dot(jnp.concatenate([p[rows] for p in parts], axis=0), to_cell[...])
     ux, uy, uz, ue = (got[p * ny:(p + 1) * ny] for p in range(4))
     own_cc[0] = cells(ux)
@@ -265,20 +276,19 @@
     spot_cb = CB.at[i, pl.ds(2 * j, 2), :]
 
     each(2, "wait_recv")
-    v1 = [V1[m] for m in range(nm)]
-    v2 = [None] * nm
-    for m in range(1, nm - 1):
-        around = flow(gxu[m - 1], gxu[m], gyu[m], gzu[m], v1[m - 1], v1[m], v1[m + 1], 2)
-        v2[m] = (1.0 + KEEP) * v1[m] + minv[m] * around
-    for m in range(2, nm - 2):
-        V2[m, rows, :] = v2[m][rows]
+
+    def middle_second(m):
+        T[m] = (1.0 + KEEP) * V1[m] + MINV[m] * middle_flow(m, V1)
+
+    over(1, nm - 1, middle_second)
+    V2[2:nm - 2, rows, :] = T[2:nm - 2, rows, :]
     pltpu.make_async_copy(line_cc, line_cc, g_recv.at[0]).wait()
     to_each(along_gx, line_cc, line_cc, 1)
-    total = None
-    for m in range(2, nm - 2):
-        around = flow(gxu[m - 1], gxu[m], gyu[m], gzu[m], v2[m - 1], v2[m], v2[m + 1], 2)
-        r = mdiag[m] * (v1[m] * (1.0 / OMEGA) - v2[m]) + around
-        total = r if total is None else total + r
+
+    def middle_residual(m, total):
+        return total + MDIAG[m] * (V1[m] * (1.0 / OMEGA) - T[m]) + middle_flow(m, T)
+
+    total = lax.fori_loop(2, nm - 2, middle_residual, jnp.zeros(tile, jnp.float32))
     own_cb[...] = cells(exact_dot(total[rows], to_cell[...]))
     for_others(lambda dev: pltpu.make_async_remote_copy(
         src_ref=own_cb, dst_ref=spot_cb, send_sem=g_send.at[2], recv_sem=g_recv.at[2],
@@ -307,12 +317,14 @@
     each(3, "wait_send")
     pltpu.make_async_copy(CB, CB, g_recv.at[2]).wait()
     b = CB[...] * cinv
-    v = b
-    for step in range(SWEEPS - 1):
+
+    def coarse(step, v):
         around = cxl * before(v) + cx * after(v)
         around = around + cyl * shift(v, 1, 1) + cy * shift(v, -1, 1)
         around = around + czl * shift(v, 1, 2) + cz * shift(v, -1, 2)
-        v = KEEP * v + b + around
+        return KEEP * v + b + around
+
+    v = lax.fori_loop(1, SWEEPS, coarse, b)
     CR[1:gx + 1, 8:8 + v.shape[1], :] = v
 
     near = [CR[i + p, pl.ds(7 + 2 * j + c, 1), :] for p in range(3) for c in range(4)]
@@ -321,17 +333,19 @@
         jnp.concatenate([jnp.broadcast_to(near[4 * p + c:4 * p + c + 1], (4, nz)) for c in range(4)], axis=0)
         for p in range(3)
     ]
-    w = [V2[m] + near[m // 2] for m in range(nm)]
-    v3 = [None] * nm
-    for m in range(1, nm - 1):
-        around = flow(gxu[m - 1], gxu[m], gyu[m], gzu[m], w[m - 1], w[m], w[m + 1], 2)
-        v3[m] = KEEP * w[m] + v1[m] + minv[m] * around
-    f = [None] * nk
-    for x in range(2, nk - 2):
-        f[x] = u2[x] + v3[(x + 1) // 2]
-    for x in range(3, nk - 3):
-        around = flow(hx[x - 1], hx[x], hy[x], hz[x], f[x - 1], f[x], f[x + 1], 1)
-        out_ref[x - 3] = (KEEP * f[x] + u1[x] + inv[x] * around)[rows]
+    for m in range(nm):
+        T[m] = V2[m] + near[m // 2]
+
+    def middle_up(m):
+        v3 = KEEP * T[m] + V1[m] + MINV[m] * middle_flow(m, T)
+        U3[2 * m - 1] = U2[2 * m - 1] + v3
+        U3[2 * m] = U2[2 * m] + v3
+
+    def fine_up(x):
+        out_ref[x - 3] = (KEEP * U3[x] + U1[x] + INV[x] * fine_flow(x, U3))[rows]
+
+    over(1, nm - 1, middle_up)
+    over(3, nk - 3, fine_up)
 
     for which, amount in enumerate((bytes_cy, bytes_cx, bytes_cb)):
         pltpu.make_async_copy(amount, amount, g_send.at[which]).wait()
@@ -374,7 +388,7 @@
             pltpu.SemaphoreType.DMA((3,)),
             pltpu.SemaphoreType.DMA((3,)),
             pltpu.SemaphoreType.DMA((3,)),
-        ],
+        ] + [pltpu.VMEM((nx + 6, deep, nz), f32)] * 9 + [pltpu.VMEM((nx // 2 + 4, deep, nz), f32)] * 7,
         compiler_params=pltpu.CompilerParams(
             collective_id=0, has_side_effects=True, vmem_limit_bytes=48 * 1024 * 1024
         ),

time: 21.8 us -> 24.5 us (1.12)
  Pallas kernels: 21 us -> 23.7 us
    pallas_call x1, Pallas kernels: 21 us -> 23.7 us  [shards(): pl.pallas_call(functools.partial(kernel, gx, gy, nx, ny), out_shape=jax.S...]
where the time goes in v6:
time: 24.5 us; the launch traced here: 24.3 us
  Pallas kernels  23.7 us (97%)
  local copies, waits for them, and re-layouts  0.63 us (3%)
    pallas_call x1, Pallas kernels, shards(): pl.pallas_call(functools.partial(kernel, gx, gy, nx, ny), out_shape=jax.S...  23.7 us
    unnamed x1, local copies, waits for them, and re-layouts  0.63 us

profile of v6, /device:TPU:0, one launch (start us, length us, event | category | flops | bytes accessed | tf_op | source)
XLA Modules:
  0.0 24.3 jit_solution(3182369678957453016)
XLA Ops:
  0.0 23.7 %shard_map.37 = f32[4,8,512]{2,1,0:T(8,128)S(1)} custom-call(f32[4,8,512]{2,1,0:T(8,128)} %rhs_hbm.1, s32[4,8,512]{2,1,0:T(8,128)} %lab_hbm.1, f32[3]{0:T(128)} %tab_hbm.1), custom_call_target="tpu_custom_call" | custom-call | tf_op jit(solution)/shard_map/pallas_call | solution.py:360
  23.7 0.6 %copy.5 = f32[4,8,512]{2,1,0:T(8,128)} copy(f32[4,8,512]{2,1,0:T(8,128)S(1)} %shard_map.37) | data formatting | bytes 131072

commit v7 on v4

--- a/solution.py
+++ b/solution.py
@@ -63,24 +63,23 @@
     return out[:n] + out[n:2 * n] + out[2 * n:]
 
 
-def kernel(gx, gy, nx, ny, rhs_hbm, lab_hbm, tab_hbm, out_ref, K, R, V1, V2, CC, CB, CR, own_cc, own_cb,
-           bytes_cy, bytes_cx, bytes_cb, lab_ref, tab_ref, to_cell, to_lane, send, recv, g_send, g_recv, fetch):
+def kernel(gx, gy, nx, ny, rhs_hbm, lab_hbm, tab_hbm, out_ref, L, R, V1, V2, CC, CB, CR, own_cc, own_cb,
+           bytes_cy, bytes_cx, bytes_cb, tab_ref, to_cell, to_lane, send, recv, g_send, g_recv, fetch):
     i = lax.axis_index("gx")
     j = lax.axis_index("gy")
     n = gx * gy
     me = i * gy + j
-    nz = lab_ref.shape[2]
+    nz = L.shape[2]
     mx = nx // 2
     tile = (2 * ROW0 + ny, nz)
     rows = slice(ROW0, ROW0 + ny)
 
-    get_lab = pltpu.make_async_copy(lab_hbm, lab_ref, fetch.at[0])
+    get_lab = pltpu.make_async_copy(lab_hbm, L.at[3:3 + nx, rows, :], fetch.at[0])
     get_tab = pltpu.make_async_copy(tab_hbm, tab_ref, fetch.at[1])
     get_rhs = pltpu.make_async_copy(rhs_hbm, R.at[2:2 + nx, rows, :], fetch.at[2])
-    get_lab.start()
     get_tab.start()
 
-    K[...] = jnp.full(K.shape, TINY, jnp.float32)
+    L[...] = jnp.full(L.shape, -1, jnp.int32)
     for buf in (R, V1, V2):
         buf[...] = jnp.zeros(buf.shape, jnp.float32)
 
@@ -102,7 +101,54 @@
 
     barrier = pltpu.get_barrier_semaphore()
     for_others(lambda dev: pl.semaphore_signal(barrier, inc=1, device_id=dev, device_id_type=MESH))
+    get_lab.start()
     get_rhs.start()
+
+    pl.semaphore_wait(barrier, n - 1)
+
+    def there(dx, dy):
+        ok = None
+        for at, d, size in ((i, dx, gx), (j, dy, gy)):
+            if d:
+                c = (at < size - 1) if d > 0 else (at > 0)
+                ok = c if ok is None else jnp.logical_and(ok, c)
+        return ok
+
+    def halo_copy(buf, whole, which, d, x0, cx, y0, cy, wx, wy, corner_x, corner_y):
+        dx, dy = DIRECTIONS[d]
+        both = dx != 0 and dy != 0
+        sx, tx, lx = span(dx, corner_x if both else wx, cx, x0)
+        sy, ty, ly = span(dy, corner_y if both else wy, cy, y0)
+        return pltpu.make_async_remote_copy(
+            src_ref=(
+                buf.at[sx:sx + lx, sy:sy + ly, :] if whole is None
+                else whole.at[sx - x0:sx - x0 + lx, sy - y0:sy - y0 + ly, :]
+            ),
+            dst_ref=buf.at[tx:tx + lx, ty:ty + ly, :],
+            send_sem=send.at[which, d],
+            recv_sem=recv.at[which, d],
+            device_id=(i + dx, j + dy),
+            device_id_type=MESH,
+        )
+
+    halos = {
+        0: (L, lab_hbm, 3, nx, ROW0, ny, 3, 3, 2, 2),
+        1: (R, rhs_hbm, 2, nx, ROW0, ny, 2, 2, 1, 1),
+        2: (V1, None, 2, mx, ROW0, ny, 2, 4, 1, 2),
+        3: (V2, None, 2, mx, ROW0, ny, 2, 4, 1, 2),
+    }
+
+    def each(which, what):
+        for d, (dx, dy) in enumerate(DIRECTIONS):
+            sign = -1 if what == "wait_recv" else 1
+
+            @pl.when(there(sign * dx, sign * dy))
+            def _():
+                buf, whole, *sizes = halos[which]
+                getattr(halo_copy(buf, whole, which, d, *sizes), what)()
+
+    each(0, "start")
+    each(1, "start")
 
     z = lax.broadcasted_iota(jnp.int32, (nz, nz // 4), 0)
     q = lax.broadcasted_iota(jnp.int32, (nz, nz // 4), 1)
@@ -112,55 +158,6 @@
     to_lane[...] = jnp.where((z >> 2) == q, 1.0, 0.0).astype(jnp.bfloat16)
     CR[...] = jnp.zeros(CR.shape, jnp.float32)
 
-    get_lab.wait()
-    get_tab.wait()
-    t0, t1, t2 = tab_ref[0], tab_ref[1], tab_ref[2]
-    labels = lab_ref[...]
-    K[3:3 + nx, rows, :] = jnp.where(labels == 0, t0, jnp.where(labels == 1, t1, t2))
-    get_rhs.wait()
-    pl.semaphore_wait(barrier, n - 1)
-
-    def there(dx, dy):
-        ok = None
-        for at, d, size in ((i, dx, gx), (j, dy, gy)):
-            if d:
-                c = (at < size - 1) if d > 0 else (at > 0)
-                ok = c if ok is None else jnp.logical_and(ok, c)
-        return ok
-
-    def halo_copy(buf, which, d, x0, cx, y0, cy, wx, wy, corner_x, corner_y):
-        dx, dy = DIRECTIONS[d]
-        both = dx != 0 and dy != 0
-        sx, tx, lx = span(dx, corner_x if both else wx, cx, x0)
-        sy, ty, ly = span(dy, corner_y if both else wy, cy, y0)
-        return pltpu.make_async_remote_copy(
-            src_ref=buf.at[sx:sx + lx, sy:sy + ly, :],
-            dst_ref=buf.at[tx:tx + lx, ty:ty + ly, :],
-            send_sem=send.at[which, d],
-            recv_sem=recv.at[which, d],
-            device_id=(i + dx, j + dy),
-            device_id_type=MESH,
-        )
-
-    halos = {
-        0: (K, 3, nx, ROW0, ny, 3, 3, 2, 2),
-        1: (R, 2, nx, ROW0, ny, 2, 2, 1, 1),
-        2: (V1, 2, mx, ROW0, ny, 2, 4, 1, 2),
-        3: (V2, 2, mx, ROW0, ny, 2, 4, 1, 2),
-    }
-
-    def each(which, what):
-        for d, (dx, dy) in enumerate(DIRECTIONS):
-            sign = -1 if what == "wait_recv" else 1
-
-            @pl.when(there(sign * dx, sign * dy))
-            def _():
-                buf, *sizes = halos[which]
-                getattr(halo_copy(buf, which, d, *sizes), what)()
-
-    each(0, "start")
-    each(1, "start")
-
     row = lax.broadcasted_iota(jnp.int32, tile, 0)
     lane = lax.broadcasted_iota(jnp.int32, tile, 1)
     odd_row = (row & 1) == 1
@@ -181,9 +178,17 @@
     faces = faces + one((row == ROW0) & (j == 0)) + one((row == ROW0 + ny - 1) & (j == gy - 1))
     x_faces = {3: one(i == 0), 2 + nx: one(i == gx - 1)}
 
+    get_lab.wait()
+    get_tab.wait()
+    t0, t1, t2 = tab_ref[0], tab_ref[1], tab_ref[2]
     each(0, "wait_recv")
+
+    def conduct(label):
+        k = jnp.where(label == 0, t0, jnp.where(label == 1, t1, t2))
+        return jnp.where(label < 0, TINY, k)
+
     nk = nx + 6
-    k = [K[x] for x in range(nk)]
+    k = [conduct(L[x]) for x in range(nk)]
 
     hx = [harmonic(k[x], k[x + 1]) for x in range(nk - 1)]
     hy, hz, edge, diag, inv = ([None] * nk for _ in range(5))
@@ -214,6 +219,7 @@
     for m in range(2, nm - 2):
         middle(m)
 
+    get_rhs.wait()
     each(1, "wait_recv")
     u1, u2 = [None] * nk, [None] * nk
     for x in range(1, nk - 1):
@@ -352,7 +358,7 @@
         ],
         out_specs=pl.BlockSpec(memory_space=pltpu.VMEM),
         scratch_shapes=[
-            pltpu.VMEM((nx + 6, deep, nz), f32),
+            pltpu.VMEM((nx + 6, deep, nz), jnp.int32),
             pltpu.VMEM((nx + 4, deep, nz), f32),
             pltpu.VMEM((nx // 2 + 4, deep, nz), f32),
             pltpu.VMEM((nx // 2 + 4, deep, nz), f32),
@@ -364,7 +370,6 @@
             pltpu.VMEM((gy - 1, 4, 2, cz), f32),
             pltpu.VMEM((gx - 1, 4, cy, cz), f32),
             pltpu.VMEM((n - 1, 2, cz), f32),
-            pltpu.VMEM((nx, ny, nz), jnp.int32),
             pltpu.SMEM((3,), f32),
             pltpu.VMEM((nz, cz), jnp.bfloat16),
             pltpu.VMEM((cz, nz), jnp.bfloat16),

time: 21.9 us -> 22 us (level)
  Pallas kernels: 21 us -> 21.3 us
where the time goes in v7:
time: 22 us; the launch traced here: 21.9 us
  Pallas kernels  21.3 us (97%)
  local copies, waits for them, and re-layouts  0.63 us (3%)
    pallas_call x1, Pallas kernels, shards(): pl.pallas_call(functools.partial(kernel, gx, gy, nx, ny), out_shape=jax.S...  21.3 us
    unnamed x1, local copies, waits for them, and re-layouts  0.63 us

profile of v7, /device:TPU:0, one launch (start us, length us, event | category | flops | bytes accessed | tf_op | source)
XLA Modules:
  0.0 21.9 jit_solution(3189557026681094650)
XLA Ops:
  0.0 21.3 %shard_map.37 = f32[4,8,512]{2,1,0:T(8,128)S(1)} custom-call(f32[4,8,512]{2,1,0:T(8,128)} %rhs_hbm.1, s32[4,8,512]{2,1,0:T(8,128)} %lab_hbm.1, f32[3]{0:T(128)} %tab_hbm.1), custom_call_target="tpu_custom_call" | custom-call | tf_op jit(solution)/shard_map/pallas_call | solution.py:351
  21.3 0.6 %copy.5 = f32[4,8,512]{2,1,0:T(8,128)} copy(f32[4,8,512]{2,1,0:T(8,128)S(1)} %shard_map.37) | data formatting | bytes 131072

commit v8 on v4

--- a/solution.py
+++ b/solution.py
@@ -104,20 +104,11 @@
     for_others(lambda dev: pl.semaphore_signal(barrier, inc=1, device_id=dev, device_id_type=MESH))
     get_rhs.start()
 
-    z = lax.broadcasted_iota(jnp.int32, (nz, nz // 4), 0)
-    q = lax.broadcasted_iota(jnp.int32, (nz, nz // 4), 1)
-    to_cell[...] = jnp.where(((z >> 2) == q) & ((z & 1) == 0), 1.0, 0.0).astype(jnp.bfloat16)
-    q = lax.broadcasted_iota(jnp.int32, (nz // 4, nz), 0)
-    z = lax.broadcasted_iota(jnp.int32, (nz // 4, nz), 1)
-    to_lane[...] = jnp.where((z >> 2) == q, 1.0, 0.0).astype(jnp.bfloat16)
-    CR[...] = jnp.zeros(CR.shape, jnp.float32)
-
     get_lab.wait()
     get_tab.wait()
     t0, t1, t2 = tab_ref[0], tab_ref[1], tab_ref[2]
     labels = lab_ref[...]
     K[3:3 + nx, rows, :] = jnp.where(labels == 0, t0, jnp.where(labels == 1, t1, t2))
-    get_rhs.wait()
     pl.semaphore_wait(barrier, n - 1)
 
     def there(dx, dy):
@@ -159,7 +150,16 @@
                 getattr(halo_copy(buf, which, d, *sizes), what)()
 
     each(0, "start")
+    get_rhs.wait()
     each(1, "start")
+
+    z = lax.broadcasted_iota(jnp.int32, (nz, nz // 4), 0)
+    q = lax.broadcasted_iota(jnp.int32, (nz, nz // 4), 1)
+    to_cell[...] = jnp.where(((z >> 2) == q) & ((z & 1) == 0), 1.0, 0.0).astype(jnp.bfloat16)
+    q = lax.broadcasted_iota(jnp.int32, (nz // 4, nz), 0)
+    z = lax.broadcasted_iota(jnp.int32, (nz // 4, nz), 1)
+    to_lane[...] = jnp.where((z >> 2) == q, 1.0, 0.0).astype(jnp.bfloat16)
+    CR[...] = jnp.zeros(CR.shape, jnp.float32)
 
     row = lax.broadcasted_iota(jnp.int32, tile, 0)
     lane = lax.broadcasted_iota(jnp.int32, tile, 1)

time: 21.9 us -> 21.8 us (level)
  no operation moved by 1% of the time
where the time goes in v8:
time: 21.8 us; the launch traced here: 21.7 us
  Pallas kernels  21 us (96%)
  local copies, waits for them, and re-layouts  0.63 us (3%)
    pallas_call x1, Pallas kernels, shards(): pl.pallas_call(functools.partial(kernel, gx, gy, nx, ny), out_shape=jax.S...  21 us
    unnamed x1, local copies, waits for them, and re-layouts  0.63 us

profile of v8, /device:TPU:0, one launch (start us, length us, event | category | flops | bytes accessed | tf_op | source)
XLA Modules:
  0.0 21.7 jit_solution(15347311617445260146)
XLA Ops:
  0.0 21.0 %shard_map.37 = f32[4,8,512]{2,1,0:T(8,128)S(1)} custom-call(f32[4,8,512]{2,1,0:T(8,128)} %rhs_hbm.1, s32[4,8,512]{2,1,0:T(8,128)} %lab_hbm.1, f32[3]{0:T(128)} %tab_hbm.1), custom_call_target="tpu_custom_call" | custom-call | tf_op jit(solution)/shard_map/pallas_call | solution.py:345
  21.1 0.6 %copy.5 = f32[4,8,512]{2,1,0:T(8,128)} copy(f32[4,8,512]{2,1,0:T(8,128)S(1)} %shard_map.37) | data formatting | bytes 131072
